TPU v7x, 32 devices: a whole 2x2x4 slice. The times are simulated.
32 devices in a mesh: seq: 8 (over y, x, core), head: 4 (over z).
Axes of the slice: x: 2, y: 2, z: 4, core: 2. Of those that a mesh axis runs over, the one named last changes fastest.
Arguments:
- hidden: bfloat16 [4096, 4096], P(('seq', 'head')), may hold values from -6 to 6
- masked: int32 [4096], P(('seq', 'head')), may hold values 0 or 1
- mask_embed: bfloat16 [4096], replicated, may hold values from -6 to 6
- in_gain: float32 [4096], replicated, may hold values from 0.5 to 1.5
- w_gate: bfloat16 [4096, 4096], P(None, 'head'), may hold values from -0.09375 to 0.09375
- w_value: bfloat16 [4096, 4096], P(None, 'head'), may hold values from -0.09375 to 0.09375
- w_step: bfloat16 [4096, 64], P(None, 'head'), may hold values from -0.09375 to 0.09375
- w_bc: bfloat16 [4096, 256], replicated, may hold values from -0.0078125 to 0.0078125
- dt_bias_forward: float32 [64], P('head'), may hold values from -1 to 1
- dt_bias_reverse: float32 [64], P('head'), may hold values from -1 to 1
- rate_forward: float32 [64], P('head'), as said below
- rate_reverse: float32 [64], P('head'), as said below
- skip_forward: float32 [64], P('head'), may hold values from 0.5 to 1.5
- skip_reverse: float32 [64], P('head'), may hold values from 0.5 to 1.5
- out_gain: float32 [4096], P('head'), may hold values from 0.1 to 1.9
- w_out: bfloat16 [4096, 4096], P('head'), may hold values from -0.09375 to 0.09375
Outputs:
- mixed: bfloat16 [4096, 4096], P(('seq', 'head'))
Inputs may be any that keep to these rules, and one draw needn't show every extreme that they name: `rate_forward`: positive decay rates of the 64 heads, each at most 0.05 a position. `rate_reverse`: positive decay rates of the 64 heads, each at most 0.05 a position.
All inputs are finite; a program needn't handle non-finite values. No bound on the sum of `masked` on one device may be relied on, other than what follows from the above.
Results may differ from a plain program's by a relative error of at most 0.014.
The roundings to bfloat16 on the way count: a program that leaves them out, or rounds other values in their place, can miss the bound.
Values may be sent and summed in bfloat16 or wider, within the bound.
A program may use at most 128 MiB of HBM per device.

v0:
```python
import jax
import jax.numpy as jnp
from jax import lax
from jax.sharding import PartitionSpec as P

HEADS = 64
HEAD_DIM = 64
STATE = 128
BLOCK = 256


epsilon = 1e-05


def prefix_2(part, axis, combine, identity, reverse):
    count = lax.axis_size(axis)
    place = lax.axis_index(axis)
    ahead = count - 1 - place if reverse else place
    gathered = jax.tree.map(lambda a: lax.all_gather(a, axis), part)
    state = jax.tree.map(lambda a, e: jnp.zeros_like(a) + jnp.asarray(e, a.dtype), part, identity)

    def one(hop, state):
        source = count - 1 - hop if reverse else hop
        return combine(
            state, jax.tree.map(lambda a: lax.dynamic_index_in_dim(a, source, 0, False), gathered)
        )

    return lax.fori_loop(0, ahead, one, state)


def block_terms(values, b_rows, c_rows, steps_dt, rates):
    row_count, head_count, head_width = values.shape
    block_count = row_count // BLOCK
    val_blk = values.reshape(block_count, BLOCK, head_count, head_width)
    b_blk = b_rows.reshape(block_count, BLOCK, STATE)
    c_blk = c_rows.reshape(block_count, BLOCK, STATE)
    step_blk = steps_dt.reshape(block_count, BLOCK, head_count)
    cumul = jnp.cumsum(-rates[None, None, :] * step_blk, axis=1)
    cumul_heads = jnp.swapaxes(cumul, 1, 2)
    differ = cumul_heads[:, :, :, None] - cumul_heads[:, :, None, :]
    tri_mask = jnp.arange(BLOCK)[:, None] >= jnp.arange(BLOCK)[None, :]
    weights = (
        jnp.exp(jnp.where(tri_mask, differ, -jnp.inf)) * jnp.swapaxes(step_blk, 1, 2)[:, :, None, :]
    )
    scores = jnp.einsum("btn,bsn->bts", c_blk, b_blk, preferred_element_type=jnp.float32)
    mixing = (scores[:, None] * weights).astype(jnp.bfloat16)
    inside = jnp.einsum("bhts,bshp->bthp", mixing, val_blk, preferred_element_type=jnp.float32)
    to_end = jnp.exp(cumul[:, -1:, :] - cumul) * step_blk
    scaled = (val_blk.astype(jnp.float32) * to_end[..., None]).astype(jnp.bfloat16)
    block_states = jnp.einsum("bshp,bsn->bhpn", scaled, b_blk, preferred_element_type=jnp.float32)
    decays = jnp.exp(cumul[:, -1, :])
    starts = []
    prefix = []
    running = jnp.zeros(block_states.shape[1:], jnp.float32)
    product = jnp.ones((head_count,), jnp.float32)
    for block_index in range(block_count):
        starts.append(running)
        prefix.append(product)
        running = decays[block_index][:, None, None] * running + block_states[block_index]
        product = product * decays[block_index]
    return ((inside, cumul, c_blk, jnp.stack(starts), jnp.stack(prefix)), running, product)


def block_output(terms, entering, values, skip_gain):
    inside, cumul, c_blk, starts, prefix = terms
    states = starts + prefix[:, :, None, None] * entering[None]
    carried = jnp.einsum(
        "btn,bhpn->bthp", c_blk, states.astype(jnp.bfloat16), preferred_element_type=jnp.float32
    )
    carried = carried * jnp.exp(cumul)[..., None]
    row_count, head_count, head_width = values.shape
    total = (inside + carried).reshape(row_count, head_count, head_width) + skip_gain[
        None, :, None
    ] * values.astype(jnp.float32)
    return total.reshape(row_count, head_count * head_width)


def combine_pairs(earlier, later):
    return (earlier[0] * later[0], later[0][:, None, None] * earlier[1] + later[1])


def on_device(
    hidden,
    masked,
    mask_embed,
    in_gain,
    w_gate,
    w_value,
    w_step,
    w_bc,
    dt_bias_forward,
    dt_bias_reverse,
    rate_forward,
    rate_reverse,
    skip_forward,
    skip_reverse,
    out_gain,
    w_out,
):
    source = jnp.where(masked[:, None] == 1, mask_embed[None, :], hidden)
    source_f = source.astype(jnp.float32)
    normed = (
        source_f
        * lax.rsqrt(jnp.mean(source_f * source_f, axis=1, keepdims=True) + epsilon)
        * in_gain[None, :]
    ).astype(jnp.bfloat16)
    gathered = lax.all_gather(normed, "head", axis=0, tiled=True)
    gate_proj = jnp.dot(gathered, w_gate, preferred_element_type=jnp.float32)
    value_proj = jnp.dot(gathered, w_value, preferred_element_type=jnp.float32)
    step_proj = jnp.dot(gathered, w_step, preferred_element_type=jnp.float32)
    bc_proj = jnp.dot(gathered, w_bc, preferred_element_type=jnp.float32)
    row_count = gathered.shape[0]
    head_count = step_proj.shape[1]
    values = jax.nn.silu(value_proj).astype(jnp.bfloat16).reshape(row_count, head_count, HEAD_DIM)
    b_rows = bc_proj[:, :STATE].astype(jnp.bfloat16)
    c_rows = bc_proj[:, STATE:].astype(jnp.bfloat16)
    dt_forward = jax.nn.softplus(step_proj + dt_bias_forward[None, :])
    dt_reverse = jax.nn.softplus(step_proj + dt_bias_reverse[None, :])
    values_back = values[::-1]
    terms_forward, end_forward, decay_forward = block_terms(
        values, b_rows, c_rows, dt_forward, rate_forward
    )
    terms_reverse, end_reverse, decay_reverse = block_terms(
        values_back, b_rows[::-1], c_rows[::-1], dt_reverse[::-1], rate_reverse
    )
    identity = (jnp.ones((head_count,), jnp.float32), jnp.zeros_like(end_forward))
    enter_forward = prefix_2((decay_forward, end_forward), "seq", combine_pairs, identity, False)[1]
    enter_reverse = prefix_2((decay_reverse, end_reverse), "seq", combine_pairs, identity, True)[1]
    forward_out = block_output(terms_forward, enter_forward, values, skip_forward)
    reverse_out = block_output(terms_reverse, enter_reverse, values_back, skip_reverse)[::-1]
    gate_act = jax.nn.silu(gate_proj)
    gated_forward = forward_out * gate_act
    gated_reverse = reverse_out * gate_act
    totals = lax.psum(
        (
            jnp.sum(gated_forward * gated_forward, axis=1),
            jnp.sum(gated_reverse * gated_reverse, axis=1),
        ),
        "head",
    )
    inner_width = HEADS * HEAD_DIM
    normed_forward = (
        gated_forward * lax.rsqrt(totals[0][:, None] / inner_width + epsilon) * out_gain[None, :]
    ).astype(jnp.bfloat16)
    normed_reverse = (
        gated_reverse * lax.rsqrt(totals[1][:, None] / inner_width + epsilon) * out_gain[None, :]
    ).astype(jnp.bfloat16)
    total = lax.psum_scatter(
        jnp.dot(normed_forward, w_out, preferred_element_type=jnp.float32).astype(jnp.bfloat16),
        "head",
        scatter_dimension=0,
        tiled=True,
    ).astype(jnp.float32) + lax.psum_scatter(
        jnp.dot(normed_reverse, w_out, preferred_element_type=jnp.float32).astype(jnp.bfloat16),
        "head",
        scatter_dimension=0,
        tiled=True,
    ).astype(
        jnp.float32
    )
    return total.astype(jnp.bfloat16)


def solution(mesh):
    in_specs = (
        P(("seq", "head"), None),
        P(("seq", "head")),
        P(),
        P(),
        P(None, "head"),
        P(None, "head"),
        P(None, "head"),
        P(),
        P("head"),
        P("head"),
        P("head"),
        P("head"),
        P("head"),
        P("head"),
        P("head"),
        P("head", None),
    )
    out_specs = P(("seq", "head"), None)
    return jax.shard_map(
        on_device, mesh=mesh, in_specs=in_specs, out_specs=out_specs, check_vma=False
    )
```

profile of v0, /device:TPU:0, one launch (start us, length us, event | category | flops | bytes accessed | tf_op | source)
XLA Modules:
  0.0 419.9 jit_solution(8695590367226106143)
XLA Ops:
  6.5 0.8 broadcast_compare_fusion
  7.4 1.7 fusion.14
  9.1 2.6 fusion.16
  11.8 83.5 %all-gather.6.cloned.1.call-done = bf16[512,4096]{1,0:T(8,128)(2,1)} async-done(((bf16[128,4096]{1,0:T(8,128)(2,1)}), bf16[512,4096]{1,0:T(8,128)(2,1)}) %all-gather.6.cloned.1.call-update) | async-done | bytes 4194320 | tf_op jit(solution)/shard_map/all_gather | solution.py:107
  95.3 4.0 compare_select_fusion.1
  99.4 0.3 rev.18
  99.7 1.1 reduce-window.16
  100.9 0.2 slice_reduce_fusion
  101.1 0.7 copy_bitcast_fusion
  101.9 0.7 bitcast_exponential_fusion
  102.6 0.6 copy.94
  103.2 10.4 %multiply_convert_fusion.8 = bf16[512,1024]{1,0:T(8,128)(2,1)} fusion(bf16[512,4096]{1,0:T(8,128)(2,1)} %all-gather.6.cloned.1.call-done, bf16[4096,1024]{1,0:T(8,128)(2,1)} %param.25), kind=kOutput, calls=%fused_computation.40 | convolution fusion | flops 4297588736 | bytes 13631488 | tf_op jit(solution)/shard_map/dot_general | solution.py:109
  113.6 1.5 copy.76
  115.1 2.0 rev.15
  117.1 2.1 reshape.158
  119.3 3.4 convolution_convert_fusion.2
  122.7 0.2 rev.17
  122.9 2.3 multiply_convert_fusion.5
  125.2 0.4 fusion.20
  125.6 1.1 slice_add_fusion
  126.8 0.3 reshape_reshape.3
  127.2 0.4 copy-done.8
  127.6 1.1 reduce-window.14
  128.7 0.2 slice_reduce_fusion.1
  129.0 0.2 slice_reduce_fusion.3
  129.3 1.0 multiply_convert_fusion.7
  130.4 0.4 fusion.22
  130.8 1.0 slice_add_fusion.2
  132.2 0.2 rev.16
  132.4 8.8 %all-gather.1 = f32[8,1,16]{2,1,0:T(1,128)S(1)} all-gather(f32[1,1,16]{2,1,0:T(1,128)S(1)} %get-tuple-element.183), channel_id=1, replica_groups=mesh['seq'=8,'head'=4] {'seq'}, dimensions={0}, use_global_device_ids=true | all-gather | bytes 576 | tf_op jit(solution)/shard_map/all_gather | solution.py:19
  141.1 8.7 %all-gather = f32[8,1,16]{2,1,0:T(1,128)S(1)} all-gather(f32[1,1,16]{2,1,0:T(1,128)S(1)} %get-tuple-element.179), channel_id=1, replica_groups=mesh['seq'=8,'head'=4] {'seq'}, dimensions={0}, use_global_device_ids=true | all-gather | bytes 576 | tf_op jit(solution)/shard_map/all_gather | solution.py:19
  149.8 1.0 fusion.49
  150.9 1.0 fusion.48
  151.9 10.3 %all-gather.10.cloned.1.call-done = f32[8,16,64,128]{3,2,1,0:T(8,128)} async-done(((f32[1,16,64,128]{3,2,1,0:T(8,128)}), f32[8,16,64,128]{3,2,1,0:T(8,128)}) %all-gather.10.cloned.1.call-update) | async-done | bytes 4194320 | tf_op jit(solution)/shard_map/all_gather | solution.py:19
  162.3 8.9 %while.27 = (s32[]{:T(128)}, f32[16,64,128]{2,1,0:T(8,128)S(1)}, s32[]{:T(128)}, f32[8,16]{1,0:T(8,128)S(1)}, f32[8,16,64,128]{3,2,1,0:T(8,128)}, /*index=5*/s32[]{:T(128)}, s32[]{:T(128)}, s32[]{:T(128)}, s32[]{:T(128)}) while((s32[]{:T(128)}, f32[16,64,128]{2,1,0:T(8,128)S(1)}, s32[]{:T(128)}, f32[8,16]{1,0:T(8,128)S(1)}, ...), condition=%wide.region_11.12_spmd, body=%wide.region_10.11_spmd.sunk | while | flops 262150 | bytes 1573203 | solution.py:28
  162.3 1.2 bitcast_add_fusion.7
  163.6 1.2 bitcast_add_fusion.7
  164.8 1.2 bitcast_add_fusion.7
  166.1 1.2 bitcast_add_fusion.7
  167.3 1.2 bitcast_add_fusion.7
  168.5 1.2 bitcast_add_fusion.7
  169.8 1.2 bitcast_add_fusion.7
  171.2 0.5 fusion.30
  171.7 0.7 copy-done.2
  172.6 2.4 fusion.17
  175.0 0.3 copy.111
  175.3 0.4 copy-done.20
  175.7 1.8 multiply_add_fusion
  177.5 1.9 copy.97
  179.4 10.5 %rev.19 = f32[512,1024]{1,0:T(8,128)} reverse(f32[512,1024]{1,0:T(8,128)S(1)} %copy.97), dimensions={0} | reverse | bytes 4194304 | tf_op jit(solution)/shard_map/rev | solution.py:130
  189.9 11.0 %all-gather.8.cloned.1.call-done = f32[8,16,64,128]{3,2,1,0:T(8,128)} async-done(((f32[1,16,64,128]{3,2,1,0:T(8,128)}), f32[8,16,64,128]{3,2,1,0:T(8,128)}) %all-gather.8.cloned.1.call-update) | async-done | bytes 4194320 | tf_op jit(solution)/shard_map/all_gather | solution.py:19
  201.0 0.5 fusion.29
  201.5 0.7 copy-done.4
  202.3 3.9 bitcast_add_fusion.3
  206.2 4.9 %copy.102 = f32[2,256,16,64]{3,2,1,0:T(8,128)} copy(f32[2,256,16,64]{1,3,2,0:T(8,128)} %bitcast_add_fusion.3) | data formatting | bytes 4194304 | tf_op jit(solution)/shard_map/reshape | solution.py:72
  211.1 3.6 reshape.174
  214.7 12.3 %multiply_reduce_fusion.1 = (f32[512]{0:T(512)S(1)}, f32[512,1024]{1,0:T(8,128)}, f32[512]{0:T(512)S(1)}, f32[512,1024]{1,0:T(8,128)}) fusion(f32[512,1024]{1,0:T(8,128)S(1)} %reshape.174, bf16[512,1024]{1,0:T(8,128)(2,1)S(1)} %copy-done.7, f32[1024]{0:T(1024)S(1)} %mul.322, f32[512,1024]{1,0:T(8,128)} %rev.19, ...), kind=kOutput, calls=%fused_computation.36 | convolution fusion | flops 4301782016 | bytes 22028288 | tf_op jit(solution)/shard_map/dot_general | solution.py:108
  227.0 11.9 %all-reduce.4 = (f32[512]{0:T(512)S(1)}, f32[512]{0:T(512)S(1)}) all-reduce(f32[512]{0:T(512)S(1)} %get-tuple-element.163, f32[512]{0:T(512)S(1)} %get-tuple-element.157), channel_id=1, replica_groups=mesh['seq'=8,'head'=4] {'head'}, use_global_device_ids=true, to_apply=%region_13.14 | all-reduce | flops 1024 | bytes 8192 | tf_op jit(solution)/shard_map/psum | solution.py:134
  238.9 10.5 %convolution_convert_fusion.1 = bf16[512,4096]{1,0:T(8,128)(2,1)} fusion(bf16[1024,4096]{1,0:T(8,128)(2,1)} %param.35, f32[512,1024]{1,0:T(8,128)} %get-tuple-element.158, f32[1024]{0:T(1024)S(1)} %copy-done.21, f32[512]{0:T(512)S(1)} %add_rsqrt_fusion.1), kind=kOutput, calls=%fused_computation.7 | convolution fusion | flops 4298637312 | bytes 14686208 | tf_op jit(solution)/shard_map/dot_general | solution.py:149
  249.5 1.5 copy-done.5
  251.0 10.9 %convolution_convert_fusion = bf16[512,4096]{1,0:T(8,128)(2,1)} fusion(bf16[1024,4096]{1,0:T(8,128)(2,1)} %param.35, f32[512]{0:T(512)S(1)} %add_rsqrt_fusion, f32[1024]{0:T(1024)S(1)} %copy-done.21, f32[512,1024]{1,0:T(8,128)S(1)} %copy-done.5, f32[512,1024]{1,0:T(8,128)} %get-tuple-element.184), kind=kOutput, calls=%fused_computation.6 | convolution fusion | flops 4301258752 | bytes 16783360 | tf_op jit(solution)/shard_map/dot_general | solution.py:154
  261.9 69.1 %reduce-scatter.3.cloned.1.call-done = bf16[128,4096]{1,0:T(8,128)(2,1)} async-done(((bf16[512,4096]{1,0:T(8,128)(2,1)}), bf16[128,4096]{1,0:T(8,128)(2,1)}) %reduce-scatter.3.cloned.1.call-update) | async-done | bytes 1048592 | tf_op jit(solution)/shard_map/reduce_scatter | solution.py:148
  331.0 79.6 %reduce-scatter.5.cloned.1.call-done = bf16[128,4096]{1,0:T(8,128)(2,1)} async-done(((bf16[512,4096]{1,0:T(8,128)(2,1)}), bf16[128,4096]{1,0:T(8,128)(2,1)}) %reduce-scatter.5.cloned.1.call-update) | async-done | bytes 1048592 | tf_op jit(solution)/shard_map/reduce_scatter | solution.py:153
  410.6 2.8 add_convert_fusion
  (92 shorter events, 1.7 us)
Async XLA Ops:
  6.5 112.7 %copy-start = (bf16[4096,256]{1,0:T(8,128)(2,1)S(1)}, bf16[4096,256]{1,0:T(8,128)(2,1)}, u32[]{:S(2)}) copy-start(bf16[4096,256]{1,0:T(8,128)(2,1)} %param.27) | copy-start | bytes 6291460
  6.5 88.8 %all-gather.6.cloned.1.call-start = ((), (), s32[]{:S(2)}) async-start(), calls=%async_computation.2 | async-start | bytes 5242880 | tf_op jit(solution)/shard_map/all_gather | solution.py:107
  7.3 4.4 %copy-start.22 = (f32[16]{0:T(128)S(1)}, f32[16]{0:T(128)}, u32[]{:S(2)}) copy-start(f32[16]{0:T(128)} %param.31) | copy-start | bytes 196
  7.4 88.0 %copy-start.14 = (bf16[4096,16]{0,1:T(8,128)(2,1)S(1)}, bf16[4096,16]{0,1:T(8,128)(2,1)}, u32[]{:S(2)}) copy-start(bf16[4096,16]{0,1:T(8,128)(2,1)} %param.26) | copy-start | bytes 393220
  7.4 88.0 %copy-start.17 = (f32[16]{0:T(128)S(1)}, f32[16]{0:T(128)}, u32[]{:S(2)}) copy-start(f32[16]{0:T(128)} %param.28) | copy-start | bytes 196
  7.4 88.0 %copy-start.18 = (f32[16]{0:T(128)S(1)}, f32[16]{0:T(128)}, u32[]{:S(2)}) copy-start(f32[16]{0:T(128)} %param.29) | copy-start | bytes 196
  11.7 150.5 %all-gather.10.cloned.1.call-start = ((), (), s32[]{:S(2)}) async-start(), calls=%async_computation.5 | async-start | bytes 4718592 | tf_op jit(solution)/shard_map/all_gather | solution.py:19
  99.6 3.6 copy-start.12
  125.2 1.6 copy-start.23
  126.8 0.8 copy-start.8
  126.8 74.1 %all-gather.8.cloned.1.call-start = ((), (), s32[]{:S(2)}) async-start(), calls=%async_computation.3 | async-start | bytes 4718592 | tf_op jit(solution)/shard_map/all_gather | solution.py:19
  127.1 3.7 copy-start.3
  130.4 1.5 copy-start.19
  130.4 1.7 copy-start.13
  130.4 1.7 copy-start.9
  131.8 199.2 %reduce-scatter.3.cloned.1.call-start = ((), (), s32[]{:S(2)}) async-start(), calls=%async_computation.4 | async-start | bytes 5242880 | tf_op jit(solution)/shard_map/reduce_scatter | solution.py:148
  162.3 9.0 %copy-start.6 = (f32[1,16,64,128]{3,2,1,0:T(8,128)S(1)}, f32[1,16,64,128]{3,2,1,0:T(8,128)}, u32[]{:S(2)}) copy-start(f32[1,16,64,128]{3,2,1,0:T(8,128)} %get-tuple-element.162) | copy-start | bytes 1572868
  171.2 1.3 copy-start.2
  171.2 1.4 copy-start.11
  171.2 1.4 copy-start.15
  171.2 1.4 copy-start.16
  175.0 0.7 copy-start.20
  201.0 1.2 copy-start.4
  201.0 1.3 copy-start.10
  211.1 3.6 copy-start.7
  214.7 24.2 %copy-start.21 = (f32[1024]{0:T(1024)S(1)}, f32[1024]{0:T(1024)}, u32[]{:S(2)}) copy-start(f32[1024]{0:T(1024)} %param.34) | copy-start | bytes 12292
  249.4 1.6 copy-start.5
  249.5 161.1 %reduce-scatter.5.cloned.1.call-start = ((), (), s32[]{:S(2)}) async-start(), calls=%async_computation.6 | async-start | bytes 5242880 | tf_op jit(solution)/shard_map/reduce_scatter | solution.py:153
  261.9 151.4 %copy-start.1 = (bf16[4096,256]{1,0:T(8,128)(2,1)S(1)}, bf16[4096,256]{1,0:T(8,128)(2,1)}, u32[]{:S(2)}) copy-start(bf16[4096,256]{1,0:T(8,128)(2,1)} %param.27) | copy-start | bytes 6291460
Sparse Core Ops, SparseCore 0:
  11.8 83.4 all-gather.5
  126.9 35.2 all-gather.9
  164.1 36.7 all-gather.7
  249.6 81.3 reduce-scatter.2
  333.2 77.2 reduce-scatter.4
where the time goes:
time: 421 us; the launch traced here: 420 us
  waiting for transfers between devices  254 us (60%)
  matrix products  61.7 us (15%)
  local copies, waits for them, and re-layouts  33.5 us (8%)
  blocking collectives  29.3 us (7%)
  other arithmetic  27.5 us (7%)
  between operations  13.6 us (3%)
    all_gather x1, waiting for transfers between devices, on_device(): gathered = lax.all_gather(normed, 'head', axis=0, tiled=True)  83.5 us
    reduce_scatter x1, waiting for transfers between devices, on_device(): lax.psum_scatter(jnp.dot(normed_reverse, w_out, preferred_element_type=jn...  79.6 us
    reduce_scatter x1, waiting for transfers between devices, on_device(): lax.psum_scatter(jnp.dot(normed_forward, w_out, preferred_element_type=jn...  69.1 us
    all_gather x2, waiting for transfers between devices, prefix_2(): gathered = jax.tree.map(lambda a: lax.all_gather(a, axis), part)  21.3 us
    all_gather x2, blocking collectives, prefix_2(): gathered = jax.tree.map(lambda a: lax.all_gather(a, axis), part)  17.4 us
    dot_general x1, matrix products, on_device(): gate_proj = jnp.dot(gathered, w_gate, preferred_element_type=jnp.float32)  12.3 us
    psum x1, blocking collectives, on_device(): lax.psum((jnp.sum(gated_forward * gated_forward, axis=1), jnp.sum(gated_r...  11.9 us
    dot_general x1, matrix products, on_device(): jnp.dot(normed_reverse, w_out, preferred_element_type=jnp.float32)  10.9 us
  transfers between devices with their start and end apart: 5, of which 5 were waited for; matrix products, arithmetic and copies ran while one was open for 10% of the time, Pallas kernels for 0%

commit v1 on v0

v1 whole, which is shorter than its diff:
```python
import jax
import jax.numpy as jnp
from jax import lax
from jax.sharding import PartitionSpec as P

HEADS = 64
HEAD_DIM = 64
STATE = 128
BLOCK = 256

epsilon = 1e-05
bf16 = jnp.bfloat16
f32 = jnp.float32


def dot(a, b):
    return jnp.dot(a, b, preferred_element_type=f32)


def direction_terms(values, b_blk, scores, steps_dt, rates, reverse):
    block_count, size, head_count, _ = values.shape
    step_blk = steps_dt.reshape(block_count, size, head_count)
    logd = -rates * step_blk
    at = jnp.arange(size)
    keep = at[:, None] <= at[None, :] if reverse else at[:, None] >= at[None, :]
    cum = jnp.einsum(
        "ts,bsh->bth", keep.astype(f32), logd, precision=lax.Precision.HIGHEST
    )
    total = cum[:, 0] if reverse else cum[:, -1]
    cum_h = jnp.swapaxes(cum, 1, 2)
    differ = cum_h[:, :, :, None] - cum_h[:, :, None, :]
    weights = (
        jnp.exp(jnp.where(keep, differ, -jnp.inf)) * jnp.swapaxes(step_blk, 1, 2)[:, :, None, :]
    )
    mixing = (scores[:, None] * weights).astype(bf16)
    inside = jnp.einsum("bhts,bshp->bthp", mixing, values, preferred_element_type=f32)
    to_end = jnp.exp(total[:, None] - cum) * step_blk
    scaled = (values.astype(f32) * to_end[..., None]).astype(bf16)
    states = jnp.einsum("bshp,bsn->bhpn", scaled, b_blk, preferred_element_type=f32)
    order = range(block_count - 1, -1, -1) if reverse else range(block_count)
    starts, prefix = [None] * block_count, [None] * block_count
    running, product = jnp.zeros_like(states[0]), jnp.zeros_like(total[0])
    for i in order:
        starts[i], prefix[i] = running, product
        running = jnp.exp(total[i])[:, None, None] * running + states[i]
        product = product + total[i]
    return inside, cum, jnp.stack(starts), jnp.stack(prefix), running, product


def entering(gathered, logs, place, reverse):
    count = gathered.shape[0]
    at = jnp.arange(count)
    if reverse:
        between = (at[None, :] < at[:, None]) & (at[None, :] > place)
        used = at > place
    else:
        between = (at[None, :] > at[:, None]) & (at[None, :] < place)
        used = at < place
    decay = jnp.sum(jnp.where(between[:, :, None], logs[None], 0.0), axis=1)
    factor = jnp.where(used[:, None], jnp.exp(decay), 0.0)
    return jnp.sum(factor[:, :, None, None] * gathered.astype(f32), axis=0)


def on_device(
    hidden, masked, mask_embed, in_gain, w_gate, w_value, w_step, w_bc,
    dt_bias_forward, dt_bias_reverse, rate_forward, rate_reverse,
    skip_forward, skip_reverse, out_gain, w_out,
):
    source = jnp.where(masked[:, None] == 1, mask_embed[None, :], hidden).astype(f32)
    normed = (
        source
        * lax.rsqrt(jnp.mean(source * source, axis=1, keepdims=True) + epsilon)
        * in_gain[None, :]
    ).astype(bf16)
    rows = lax.all_gather(normed, "head", axis=0, tiled=True)
    gate_act = jax.nn.silu(dot(rows, w_gate))
    step_proj = dot(rows, w_step)
    row_count, head_count = step_proj.shape
    block_count = row_count // BLOCK
    values = jax.nn.silu(dot(rows, w_value)).astype(bf16)
    values = values.reshape(block_count, BLOCK, head_count, HEAD_DIM)
    bc = dot(rows, w_bc).astype(bf16).reshape(block_count, BLOCK, 2 * STATE)
    b_blk, c_blk = bc[..., :STATE], bc[..., STATE:]
    scores = jnp.einsum("btn,bsn->bts", c_blk, b_blk, preferred_element_type=f32)
    dt_f = jax.nn.softplus(step_proj + dt_bias_forward)
    dt_r = jax.nn.softplus(step_proj + dt_bias_reverse)
    terms_f = direction_terms(values, b_blk, scores, dt_f, rate_forward, False)
    terms_r = direction_terms(values, b_blk, scores, dt_r, rate_reverse, True)
    ends = jnp.stack([terms_f[4], terms_r[4]]).astype(bf16)
    logs = lax.all_gather(jnp.stack([terms_f[5], terms_r[5]]), "seq")
    ends = lax.all_gather(ends, "seq")
    place = lax.axis_index("seq")
    gated = []
    for i, (terms, skip) in enumerate(((terms_f, skip_forward), (terms_r, skip_reverse))):
        inside, cum, starts, prefix = terms[:4]
        enter = entering(ends[:, i], logs[:, i], place, i == 1)
        states = (starts + jnp.exp(prefix)[:, :, None, None] * enter[None]).astype(bf16)
        carried = jnp.einsum("btn,bhpn->bthp", c_blk, states, preferred_element_type=f32)
        out = inside + carried * jnp.exp(cum)[..., None] + skip[:, None] * values.astype(f32)
        gated.append(out.reshape(row_count, -1) * gate_act)
    totals = lax.psum(jnp.stack([jnp.sum(g * g, axis=1) for g in gated]), "head")
    inner = HEADS * HEAD_DIM
    scale = lax.rsqrt(totals / inner + epsilon)
    both = gated[0] * scale[0][:, None] + gated[1] * scale[1][:, None]
    both = (both * out_gain[None, :]).astype(bf16)
    part = dot(both, w_out).astype(bf16)
    return lax.psum_scatter(part, "head", scatter_dimension=0, tiled=True)


def solution(mesh):
    head = P("head")
    in_specs = (
        P(("seq", "head"), None), P(("seq", "head")), P(), P(),
        P(None, "head"), P(None, "head"), P(None, "head"), P(),
        head, head, head, head, head, head, head, P("head", None),
    )
    return jax.shard_map(
        on_device, mesh=mesh, in_specs=in_specs,
        out_specs=P(("seq", "head"), None), check_vma=False,
    )
```

time: 421 us -> 304 us (0.72)
  waiting for transfers between devices: 254 us -> 179 us
  other arithmetic: 27.5 us -> 15.1 us
  matrix products: 61.7 us -> 49.5 us
  blocking collectives: 29.3 us -> 20.8 us
  local copies, waits for them, and re-layouts: 33.5 us -> 25.5 us
    reduce_scatter x2 -> x1, waiting for transfers between devices: 149 us -> 74.1 us  [on_device(): return lax.psum_scatter(part, 'head', scatter_dimension=0, tiled=True)]
    rev x5 -> x0, local copies, waits for them, and re-layouts: 13.1 us -> none  [the longest x1 10.5 us: on_device(): block_output(terms_reverse, enter_reverse, values_back, skip_reverse)[::-1]]
    dot_general x14, matrix products: 61.7 us -> 49.5 us  [the longest x5 38.3 us: dot(): return jnp.dot(a, b, preferred_element_type=f32)]
    add x10 -> x1, other arithmetic: 12.3 us -> 0.67 us  [direction_terms(): product = product + total[i]]
    reshape x7 -> x8, local copies, waits for them, and re-layouts: 12.8 us -> 22.2 us  [the longest x4 17 us: on_device(): gated.append(out.reshape(row_count, -1) * gate_act)]
    all_gather x2 -> x1, blocking collectives: 17.4 us -> 9.08 us  [on_device(): logs = lax.all_gather(jnp.stack([terms_f[5], terms_r[5]]), 'seq')]
    convert_element_type x4 -> x1, other arithmetic: 8.65 us -> 2.59 us  [on_device(): normed = (source * lax.rsqrt(jnp.mean(source * source, axis=1, keepdims=T...]
    all_gather x3 -> x2, waiting for transfers between devices: 105 us -> 104 us  [the longest x1 83.5 us: on_device(): rows = lax.all_gather(normed, 'head', axis=0, tiled=True)]
  transfers between devices with their start and end apart: 5 -> 3, of which waited for: 5 -> 3; matrix products, arithmetic and copies ran while one was open for 10% -> 2% of each run, Pallas kernels for 0% -> 0%
where the time goes in v1:
time: 304 us; the launch traced here: 303 us
  waiting for transfers between devices  179 us (59%)
  matrix products  49.5 us (16%)
  local copies, waits for them, and re-layouts  25.5 us (8%)
  blocking collectives  20.8 us (7%)
  other arithmetic  15.1 us (5%)
  between operations  13.5 us (4%)
    all_gather x1, waiting for transfers between devices, on_device(): rows = lax.all_gather(normed, 'head', axis=0, tiled=True)  83.5 us
    reduce_scatter x1, waiting for transfers between devices, on_device(): return lax.psum_scatter(part, 'head', scatter_dimension=0, tiled=True)  74.1 us
    dot_general x5, matrix products, dot(): return jnp.dot(a, b, preferred_element_type=f32)  38.3 us
    all_gather x1, waiting for transfers between devices, on_device(): ends = lax.all_gather(ends, 'seq')  20.9 us
    reshape x4, local copies, waits for them, and re-layouts, on_device(): gated.append(out.reshape(row_count, -1) * gate_act)  17 us
    psum x1, blocking collectives, on_device(): lax.psum(jnp.stack([jnp.sum(g * g, axis=1) for g in gated]), 'head')  11.7 us
    all_gather x1, blocking collectives, on_device(): logs = lax.all_gather(jnp.stack([terms_f[5], terms_r[5]]), 'seq')  9.08 us
    dot_general x2, matrix products, direction_terms(): jnp.einsum('bhts,bshp->bthp', mixing, values, preferred_element_type=f32)  6.53 us
  transfers between devices with their start and end apart: 3, of which 3 were waited for; matrix products, arithmetic and copies ran while one was open for 2% of the time, Pallas kernels for 0%

profile of v1, /device:TPU:0, one launch (start us, length us, event | category | flops | bytes accessed | tf_op | source)
XLA Modules:
  0.0 303.1 jit_solution(9905027285953389305)
XLA Ops:
  6.5 0.0 copy-start
  6.5 0.0 all-gather.5.cloned.1.call-start
  6.5 0.8 broadcast_compare_fusion
  7.4 0.0 copy-start.16
  7.4 0.0 copy-start.17
  7.4 1.8 fusion.16
  9.1 2.6 fusion.18
  11.7 0.0 all-gather.5.cloned.1.call-update
  11.8 0.0 all-gather.7.cloned.1.call-start
  11.8 0.0 copy-done.19
  11.8 0.0 copy-done.20
  11.9 83.5 %all-gather.5.cloned.1.call-done = bf16[512,4096]{1,0:T(8,128)(2,1)} async-done(((bf16[128,4096]{1,0:T(8,128)(2,1)}), bf16[512,4096]{1,0:T(8,128)(2,1)}) %all-gather.5.cloned.1.call-update) | async-done | bytes 4194320 | tf_op jit(solution)/shard_map/all_gather | solution.py:75
  95.4 3.6 %compare_select_fusion = (f32[512,16]{0,1:T(8,128)S(1)}, f32[512,16]{0,1:T(8,128)S(1)}) fusion(f32[16]{0:T(128)S(1)} %copy-done.16, f32[16]{0:T(128)S(1)} %copy-done.17, bf16[512,4096]{1,0:T(8,128)(2,1)} %all-gather.5.cloned.1.call-done, bf16[4096,16]{0,1:T(8,128)(2,1)S(1)} %copy-done.6), kind=kOutput, calls=%fused_computation.88 | convolution fusion | flops 67223552 | bytes 4391040 | tf_op jit(solution)/shard_map/dot_general | solution.py:17
  99.0 0.3 fusion.46
  99.3 0.2 slice_reduce_fusion.1
  99.4 0.8 slice_reduce_fusion.5
  100.2 0.3 fusion.44
  100.4 0.1 slice_reduce_fusion
  100.5 0.7 slice_reduce_fusion.3
  101.2 0.6 bitcast_exponential_fusion
  101.8 0.0 copy-done.7
  101.8 0.6 bitcast_exponential_fusion.1
  102.4 0.0 copy-done.2
  102.4 8.1 %multiply_convert_fusion.5 = bf16[512,1024]{1,0:T(8,128)(2,1)S(1)} fusion(bf16[512,4096]{1,0:T(8,128)(2,1)S(1)} %copy-done.2, bf16[4096,1024]{1,0:T(8,128)(2,1)} %param.21), kind=kOutput, calls=%fused_computation.42 | convolution fusion | flops 4297588736 | bytes 13631488 | tf_op jit(solution)/shard_map/dot_general | solution.py:17
  110.5 2.4 reshape.283
  112.9 2.8 copy.61
  115.7 3.4 %convolution_convert_fusion.1 = bf16[512,256]{1,0:T(8,128)(2,1)S(1)} fusion(bf16[512,4096]{1,0:T(8,128)(2,1)} %all-gather.5.cloned.1.call-done, bf16[4096,256]{1,0:T(8,128)(2,1)S(1)} %copy-done), kind=kOutput, calls=%fused_computation.43 | convolution fusion | flops 1073872896 | bytes 6553600 | tf_op jit(solution)/shard_map/dot_general | solution.py:17
  119.1 0.4 fusion.23
  119.6 0.4 fusion.25
  120.0 1.2 fusion.42
  121.2 0.8 pad_maximum_fusion
  122.1 0.0 all-gather.7.cloned.1.call-update
  122.1 0.0 reduce-scatter.2.cloned.1.call-start
  122.2 0.6 iota_compare_fusion
  122.9 0.6 copy.69
  123.5 0.6 copy.60
  124.1 0.7 bitcast_add_fusion.2
  124.8 9.1 %all-gather.1 = f32[8,2,16]{2,1,0:T(2,128)S(1)} all-gather(f32[1,2,16]{2,1,0:T(2,128)S(1)} %maximum_bitcast_fusion), channel_id=2, replica_groups=mesh['seq'=8,'head'=4] {'seq'}, dimensions={0}, use_global_device_ids=true | all-gather | bytes 1152 | tf_op jit(solution)/shard_map/all_gather | solution.py:90
  133.9 0.6 pad_exponential_fusion.1
  134.5 0.6 pad_exponential_fusion
  135.2 0.1 select_reduce_fusion
  135.2 0.1 select_reduce_fusion.1
  135.3 0.1 exponential_select_fusion
  135.4 0.1 exponential_select_fusion.1
  135.5 1.1 fusion.54
  136.6 20.9 %all-gather.7.cloned.1.call-done = bf16[8,2,16,64,128]{4,3,2,1,0:T(8,128)(2,1)} async-done(((bf16[1,2,16,64,128]{4,3,2,1,0:T(8,128)(2,1)}), bf16[8,2,16,64,128]{4,3,2,1,0:T(8,128)(2,1)}) %all-gather.7.cloned.1.call-update) | async-done | bytes 4194320 | tf_op jit(solution)/shard_map/all_gather | solution.py:91
  157.5 3.5 %fusion.3 = (f32[16,64,128]{2,1,0:T(8,128)}, f32[16,64,128]{2,1,0:T(8,128)S(1)}) fusion(bf16[8,2,16,64,128]{4,3,2,1,0:T(8,128)(2,1)} %all-gather.7.cloned.1.call-done, f32[8,16]{1,0:T(8,128)S(1)} %exponential_select_fusion.1, f32[8,16]{1,0:T(8,128)S(1)} %exponential_select_fusion), kind=kLoop, calls=%fused_computation.8 | loop fusion | flops 6029312 | bytes 5243904 | tf_op jit(solution)/shard_map/reduce_sum | solution.py:61
  161.0 0.0 copy-start.21
  161.1 0.5 fusion.33
  161.5 0.5 copy-done.4
  162.1 2.5 fusion.22
  164.6 3.8 %copy.77 = f32[2,256,16,64]{3,2,1,0:T(8,128)} copy(f32[2,256,16,64]{1,3,2,0:T(8,128)S(1)} %fusion.22) | data formatting | bytes 4194304 | tf_op jit(solution)/shard_map/reshape | solution.py:100
  168.4 3.5 %reshape.282 = f32[512,1024]{1,0:T(8,128)S(1)} reshape(f32[2,256,16,64]{3,2,1,0:T(8,128)} %copy.77) | data formatting | bytes 4194304 | tf_op jit(solution)/shard_map/reshape | solution.py:100
  172.0 0.0 copy-start.22
  172.0 1.7 fusion.32
  173.8 4.0 %fusion.21 = f32[2,256,16,64]{1,3,2,0:T(8,128)} fusion(bf16[2,256,16,64]{1,3,2,0:T(8,128)(2,1)S(1)} %copy.61, f32[2,256,16,64]{1,3,2,0:T(8,128)S(1)} %fusion.32, f32[2,16,256]{2,1,0:T(8,128)S(1)} %copy-done.12, f32[2,16,256]{2,1,0:T(8,128)S(1)} %copy-done.8, f32[2,256,256]{2,1,0:T(8,128)S(1)} %copy-done.5, pred[256,256]{1,0:T(8,128)(4,1)S(1)} %iota_compare_fusion.1, ...), kind=kOutput, calls=%fused_computation.32 | convolution fusion | flops 281542656 | bytes 5931072 | tf_op jit(solution)/shard_map/bhts,bshp->bthp/dot_general | solution.py:36
  177.8 4.9 %copy.76 = f32[2,256,16,64]{3,2,1,0:T(8,128)} copy(f32[2,256,16,64]{1,3,2,0:T(8,128)} %fusion.21) | data formatting | bytes 4194304 | tf_op jit(solution)/shard_map/reshape | solution.py:100
  182.6 4.8 %reshape.281 = f32[512,1024]{1,0:T(8,128)} reshape(f32[2,256,16,64]{3,2,1,0:T(8,128)} %copy.76) | data formatting | bytes 4194304 | tf_op jit(solution)/shard_map/reshape | solution.py:100
  187.5 11.5 %multiply_reduce_fusion.1 = (f32[512]{0:T(512)S(1)}, f32[512]{0:T(512)S(1)}, f32[512,1024]{1,0:T(8,128)}) fusion(f32[512,1024]{1,0:T(8,128)} %reshape.281, f32[512,1024]{1,0:T(8,128)S(1)} %reshape.282, bf16[512,4096]{1,0:T(8,128)(2,1)} %all-gather.5.cloned.1.call-done, bf16[4096,1024]{1,0:T(8,128)(2,1)} %param.20), kind=kOutput, calls=%fused_computation.40 | convolution fusion | flops 4300209152 | bytes 18878464 | tf_op jit(solution)/shard_map/dot_general | solution.py:17
  199.0 11.7 %psum.7 = f32[2,512]{1,0:T(2,128)S(1)} all-reduce(f32[2,512]{1,0:T(2,128)S(1)} %pad_maximum_fusion.1), channel_id=1, replica_groups=mesh['seq'=8,'head'=4] {'head'}, use_global_device_ids=true, to_apply=%region_7.8 | all-reduce | flops 1024 | bytes 8192 | tf_op jit(solution)/shard_map/psum | solution.py:101
  210.7 0.0 copy-done.18
  210.8 11.7 %convolution_convert_fusion = bf16[512,4096]{1,0:T(8,128)(2,1)} fusion(bf16[1024,4096]{1,0:T(8,128)(2,1)} %param.31, f32[1024]{0:T(1024)S(1)} %copy-done.18, f32[512]{0:T(512)S(1)} %bitcast.120, f32[512]{0:T(512)S(1)} %bitcast.119, f32[512,1024]{1,0:T(8,128)} %reshape.281, f32[512,1024]{1,0:T(8,128)} %get-tuple-element.31, f32[512,1024]{1,0:T(8,128)S(1)} %reshape.282), kind=kOutput, calls=%fused_computation.2 | convolution fusion | flops 4302831616 | bytes 18882560 | tf_op jit(solution)/shard_map/dot_general | solution.py:17
  222.4 0.0 reduce-scatter.2.cloned.1.call-update
  222.4 74.1 %reduce-scatter.2.cloned.1.call-done = bf16[128,4096]{1,0:T(8,128)(2,1)} async-done(((bf16[512,4096]{1,0:T(8,128)(2,1)}), bf16[128,4096]{1,0:T(8,128)(2,1)}) %reduce-scatter.2.cloned.1.call-update) | async-done | bytes 1048592 | tf_op jit(solution)/shard_map/reduce_scatter | solution.py:107
  (49 shorter events, 0.2 us)
Async XLA Ops:
  6.5 109.1 %copy-start = (bf16[4096,256]{1,0:T(8,128)(2,1)S(1)}, bf16[4096,256]{1,0:T(8,128)(2,1)}, u32[]{:S(2)}) copy-start(bf16[4096,256]{1,0:T(8,128)(2,1)} %param.23) | copy-start | bytes 6291460
  6.5 88.8 %all-gather.5.cloned.1.call-start = ((), (), s32[]{:S(2)}) async-start(), calls=%async_computation.1 | async-start | bytes 5242880 | tf_op jit(solution)/shard_map/all_gather | solution.py:75
  7.3 4.5 %copy-start.19 = (f32[16]{0:T(128)S(1)}, f32[16]{0:T(128)}, u32[]{:S(2)}) copy-start(f32[16]{0:T(128)} %param.26) | copy-start | bytes 196
  7.4 4.5 %copy-start.20 = (f32[16]{0:T(128)S(1)}, f32[16]{0:T(128)}, u32[]{:S(2)}) copy-start(f32[16]{0:T(128)} %param.27) | copy-start | bytes 196
  7.4 88.0 %copy-start.6 = (bf16[4096,16]{0,1:T(8,128)(2,1)S(1)}, bf16[4096,16]{0,1:T(8,128)(2,1)}, u32[]{:S(2)}) copy-start(bf16[4096,16]{0,1:T(8,128)(2,1)} %param.22) | copy-start | bytes 393220
  7.4 88.0 %copy-start.16 = (f32[16]{0:T(128)S(1)}, f32[16]{0:T(128)}, u32[]{:S(2)}) copy-start(f32[16]{0:T(128)} %param.25) | copy-start | bytes 196
  7.4 88.0 %copy-start.17 = (f32[16]{0:T(128)S(1)}, f32[16]{0:T(128)}, u32[]{:S(2)}) copy-start(f32[16]{0:T(128)} %param.24) | copy-start | bytes 196
  11.8 145.7 %all-gather.7.cloned.1.call-start = ((), (), s32[]{:S(2)}) async-start(), calls=%async_computation.2 | async-start | bytes 4718592 | tf_op jit(solution)/shard_map/all_gather | solution.py:91
  95.4 7.0 %copy-start.2 = (bf16[512,4096]{1,0:T(8,128)(2,1)S(1)}, bf16[512,4096]{1,0:T(8,128)(2,1)}, u32[]{:S(2)}) copy-start(bf16[512,4096]{1,0:T(8,128)(2,1)} %all-gather.5.cloned.1.call-done) | copy-start | bytes 12582916
  99.2 2.6 copy-start.7
  100.4 1.4 copy-start.9
  122.1 174.5 %reduce-scatter.2.cloned.1.call-start = ((), (), s32[]{:S(2)}) async-start(), calls=%async_computation.3 | async-start | bytes 5242880 | tf_op jit(solution)/shard_map/reduce_scatter | solution.py:107
  136.6 24.5 %copy-start.3 = (f32[1,16,64,128]{3,2,1,0:T(8,128)S(1)}, f32[1,16,64,128]{3,2,1,0:T(8,128)}, u32[]{:S(2)}) copy-start(f32[1,16,64,128]{3,2,1,0:T(8,128)} %get-tuple-element.33) | copy-start | bytes 1572868
  161.0 1.0 copy-start.4
  161.0 1.0 copy-start.10
  161.0 1.0 copy-start.11
  161.0 1.0 copy-start.13
  161.0 1.0 copy-start.15
  161.0 1.0 copy-start.21
  171.9 1.8 copy-start.5
  171.9 1.8 copy-start.8
  172.0 1.8 copy-start.12
  172.0 1.8 copy-start.14
  172.0 1.8 copy-start.22
  187.5 23.3 %copy-start.18 = (f32[1024]{0:T(1024)S(1)}, f32[1024]{0:T(1024)}, u32[]{:S(2)}) copy-start(f32[1024]{0:T(1024)} %param.30) | copy-start | bytes 12292
  222.4 74.2 %copy-start.1 = (bf16[4096,256]{1,0:T(8,128)(2,1)S(1)}, bf16[4096,256]{1,0:T(8,128)(2,1)}, u32[]{:S(2)}) copy-start(bf16[4096,256]{1,0:T(8,128)(2,1)} %param.23) | copy-start | bytes 6291460
Sparse Core Ops, SparseCore 0:
  11.9 83.4 all-gather.4
  122.2 35.2 all-gather.6
  222.6 73.9 reduce-scatter.1

commit v2 on v1

--- a/solution.py
+++ b/solution.py
@@ -1,6 +1,10 @@
+import functools
+
 import jax
 import jax.numpy as jnp
 from jax import lax
+from jax.experimental import pallas as pl
+from jax.experimental.pallas import tpu as pltpu
 from jax.sharding import PartitionSpec as P
 
 HEADS = 64
@@ -11,10 +15,280 @@
 epsilon = 1e-05
 bf16 = jnp.bfloat16
 f32 = jnp.float32
+MESH = pl.DeviceIdType.MESH
 
 
 def dot(a, b):
     return jnp.dot(a, b, preferred_element_type=f32)
+
+
+def line_barrier(axis, n):
+    me = lax.axis_index(axis)
+    barrier = pltpu.get_barrier_semaphore()
+    for other in range(1, n):
+        pl.semaphore_signal(
+            barrier, inc=1, device_id={axis: lax.rem(me + other, n)}, device_id_type=MESH
+        )
+    pl.semaphore_wait(barrier, n - 1)
+
+
+def project_kernel(
+    n, subs, hidden, masked, embed, in_gain, gate_hbm, value_hbm, step_hbm, bc_hbm,
+    gate_out, value_out, step_out, bc_out,
+    rows, w_gate, w_value, w_step, w_bc, load_sem, right_sem, left_sem, recv_sem,
+):
+    me = lax.axis_index("head")
+    loads = [
+        pltpu.make_async_copy(src, dst, load_sem.at[i])
+        for i, (src, dst) in enumerate(
+            ((bc_hbm, w_bc), (step_hbm, w_step), (value_hbm, w_value), (gate_hbm, w_gate))
+        )
+    ]
+    for load in loads:
+        load.start()
+    count = hidden.shape[0]
+    part = count // subs
+
+    def copy(chunk, sub, send_sem, target):
+        piece = rows.at[chunk, pl.ds(sub * part, part)]
+        return pltpu.make_async_remote_copy(
+            src_ref=piece, dst_ref=piece, send_sem=send_sem.at[chunk, sub],
+            recv_sem=recv_sem.at[chunk, sub],
+            device_id={"head": target}, device_id_type=MESH,
+        )
+
+    line_barrier("head", n)
+    for sub in range(subs):
+        own = pl.ds(sub * part, part)
+        source = jnp.where(masked[own, :] == 1, embed[...], hidden[own, :]).astype(f32)
+        mean = jnp.mean(source * source, axis=1, keepdims=True)
+        rows[me, own, :] = (source * lax.rsqrt(mean + epsilon) * in_gain[...]).astype(bf16)
+
+        @pl.when(me < n - 1)
+        def _():
+            copy(me, sub, right_sem, me + 1).start()
+
+        @pl.when(me > 0)
+        def _():
+            copy(me, sub, left_sem, me - 1).start()
+
+    for load in loads:
+        load.wait()
+
+    def compute(chunk):
+        x = rows[chunk]
+        at = pl.ds(pl.multiple_of(chunk * count, count), count)
+        bc_out[at, :] = dot(x, w_bc[...]).astype(bf16)
+        step_out[at, :] = dot(x, w_step[...])
+        width = w_gate.shape[1]
+        tile = 256 if width % 256 == 0 else width
+
+        @pl.loop(0, width // tile)
+        def _(i):
+            cols = pl.ds(pl.multiple_of(i * tile, tile), tile)
+            v = dot(x, w_value[:, cols])
+            value_out[at, cols] = (v * jax.nn.sigmoid(v)).astype(bf16)
+            g = dot(x, w_gate[:, cols])
+            gate_out[at, cols] = (g * jax.nn.sigmoid(g)).astype(bf16)
+
+    compute(me)
+
+    @pl.loop(1, n)
+    def _(d):
+        @pl.when(me - d >= 0)
+        def _():
+            for sub in range(subs):
+                copy(me - d, sub, right_sem, me).wait_recv()
+
+                @pl.when(me < n - 1)
+                def _():
+                    copy(me - d, sub, right_sem, me + 1).start()
+
+        @pl.when(me + d < n)
+        def _():
+            for sub in range(subs):
+                copy(me + d, sub, left_sem, me).wait_recv()
+
+                @pl.when(me > 0)
+                def _():
+                    copy(me + d, sub, left_sem, me - 1).start()
+
+        @pl.when(me - d >= 0)
+        def _():
+            compute(me - d)
+
+        @pl.when(me + d < n)
+        def _():
+            compute(me + d)
+
+    @pl.loop(0, n)
+    def _(c):
+        @pl.when((c <= me) & (me < n - 1))
+        def _():
+            for sub in range(subs):
+                copy(c, sub, right_sem, me + 1).wait_send()
+
+        @pl.when((c >= me) & (me > 0))
+        def _():
+            for sub in range(subs):
+                copy(c, sub, left_sem, me - 1).wait_send()
+
+
+def project(n, hidden, masked, mask_embed, in_gain, w_gate, w_value, w_step, w_bc):
+    count, width = hidden.shape
+    units, heads, both = w_gate.shape[1], w_step.shape[1], w_bc.shape[1]
+    subs = 2
+    total = n * count
+    vmem, any_ = pl.BlockSpec(memory_space=pltpu.VMEM), pl.BlockSpec(memory_space=pl.ANY)
+    sems = pltpu.SemaphoreType.DMA((n, subs))
+    return pl.pallas_call(
+        functools.partial(project_kernel, n, subs),
+        out_shape=(
+            jax.ShapeDtypeStruct((total, units), bf16),
+            jax.ShapeDtypeStruct((total, units), bf16),
+            jax.ShapeDtypeStruct((total, heads), f32),
+            jax.ShapeDtypeStruct((total, both), bf16),
+        ),
+        in_specs=[vmem] * 4 + [any_] * 4,
+        out_specs=(vmem,) * 4,
+        scratch_shapes=[
+            pltpu.VMEM((n, count, width), bf16),
+            pltpu.VMEM(w_gate.shape, bf16), pltpu.VMEM(w_value.shape, bf16),
+            pltpu.VMEM(w_step.shape, bf16), pltpu.VMEM(w_bc.shape, bf16),
+            pltpu.SemaphoreType.DMA((4,)), sems, sems, sems,
+        ],
+        compiler_params=pltpu.CompilerParams(
+            collective_id=0, has_side_effects=True, vmem_limit_bytes=56 * 2**20
+        ),
+    )(hidden, masked[:, None], mask_embed[None], in_gain[None], w_gate, w_value, w_step, w_bc)
+
+
+def output_kernel(
+    n, subs, inner, gated_f, gated_r, gain, w_hbm, out,
+    w_out, both, sums, held, sent, load_sem, sum_send, sum_recv, send_sem, recv_sem,
+):
+    me = lax.axis_index("head")
+    load = pltpu.make_async_copy(w_hbm, w_out, load_sem)
+    load.start()
+    count = out.shape[0]
+    part = out.shape[1] // subs
+    ones = jnp.ones((8, gated_f.shape[1]), f32)
+
+    def row_sums(ref):
+        g = ref[...]
+        return lax.dot_general(
+            ones, g * g, (((1,), (1,)), ((), ())),
+            precision=lax.Precision.HIGHEST, preferred_element_type=f32,
+        )
+
+    sums[me, 0:8, :] = row_sums(gated_f)
+    sums[me, 8:16, :] = row_sums(gated_r)
+    line_barrier("head", n)
+
+    def share(owner, target, slot):
+        return pltpu.make_async_remote_copy(
+            src_ref=sums.at[owner], dst_ref=sums.at[owner], send_sem=sum_send.at[slot],
+            recv_sem=sum_recv.at[owner], device_id={"head": target}, device_id_type=MESH,
+        )
+
+    for other in range(1, n):
+        share(me, lax.rem(me + other, n), other).start()
+    for other in range(1, n):
+        owner = lax.rem(me + other, n)
+        share(owner, owner, other).wait_recv()
+    total = jnp.sum(sums[...], axis=0)
+    scale = lax.rsqrt(total / inner + epsilon).T
+    mixed = gated_f[...] * scale[:, 0:1] + gated_r[...] * scale[:, 8:9]
+    both[...] = (mixed * gain[...]).astype(bf16)
+    load.wait()
+
+    def partial(dest, sub):
+        at = pl.ds(pl.multiple_of(dest * count, count), count)
+        return dot(both[at, :], w_out[:, pl.ds(pl.multiple_of(sub * part, part), part)])
+
+    def send(dest, sub, way, target):
+        return pltpu.make_async_remote_copy(
+            src_ref=sent.at[dest, sub], dst_ref=held.at[way, dest, sub],
+            send_sem=send_sem.at[dest, sub], recv_sem=recv_sem.at[way, dest, sub],
+            device_id={"head": target}, device_id_type=MESH,
+        )
+
+    def pass_on(dest, sub, way, first, target):
+        sent[dest, sub] = partial(dest, sub).astype(bf16)
+
+        @pl.when(jnp.logical_not(first))
+        def _():
+            send(dest, sub, way, me).wait_recv()
+            sent[dest, sub] = (
+                sent[dest, sub].astype(f32) + held[way, dest, sub].astype(f32)
+            ).astype(bf16)
+
+        send(dest, sub, way, target).start()
+
+    @pl.loop(0, (n - 1) * subs)
+    def _(i):
+        t, sub = i // subs, lax.rem(i, subs)
+
+        @pl.when((t >= me) & (me < n - 1))
+        def _():
+            pass_on(n - 1 - t + me, sub, 0, me == 0, me + 1)
+
+        @pl.when((t >= n - 1 - me) & (me > 0))
+        def _():
+            pass_on(t - (n - 1 - me), sub, 1, me == n - 1, me - 1)
+
+    @pl.loop(0, subs)
+    def _(sub):
+        cols = pl.ds(pl.multiple_of(sub * part, part), part)
+        out[:, cols] = partial(me, sub).astype(bf16)
+
+        @pl.when(me > 0)
+        def _():
+            send(me, sub, 0, me).wait_recv()
+            out[:, cols] = (out[:, cols].astype(f32) + held[0, me, sub].astype(f32)).astype(bf16)
+
+        @pl.when(me < n - 1)
+        def _():
+            send(me, sub, 1, me).wait_recv()
+            out[:, cols] = (out[:, cols].astype(f32) + held[1, me, sub].astype(f32)).astype(bf16)
+
+    @pl.loop(0, n * subs)
+    def _(i):
+        dest, sub = i // subs, lax.rem(i, subs)
+
+        @pl.when(dest != me)
+        def _():
+            send(dest, sub, 0, me).wait_send()
+
+    for other in range(1, n):
+        share(me, me, other).wait_send()
+
+
+def project_out(n, inner, gated_f, gated_r, out_gain, w_out):
+    rows, units = gated_f.shape
+    width = w_out.shape[1]
+    count = rows // n
+    subs = 4
+    vmem, any_ = pl.BlockSpec(memory_space=pltpu.VMEM), pl.BlockSpec(memory_space=pl.ANY)
+    return pl.pallas_call(
+        functools.partial(output_kernel, n, subs, inner),
+        out_shape=jax.ShapeDtypeStruct((count, width), bf16),
+        in_specs=[vmem] * 3 + [any_],
+        out_specs=vmem,
+        scratch_shapes=[
+            pltpu.VMEM(w_out.shape, bf16),
+            pltpu.VMEM((rows, units), bf16),
+            pltpu.VMEM((n, 16, rows), f32),
+            pltpu.VMEM((2, n, subs, count, width // subs), bf16),
+            pltpu.VMEM((n, subs, count, width // subs), bf16),
+            pltpu.SemaphoreType.DMA, pltpu.SemaphoreType.DMA((n,)),
+            pltpu.SemaphoreType.DMA((n,)), pltpu.SemaphoreType.DMA((n, subs)),
+            pltpu.SemaphoreType.DMA((2, n, subs)),
+        ],
+        compiler_params=pltpu.CompilerParams(
+            collective_id=1, has_side_effects=True, vmem_limit_bytes=56 * 2**20
+        ),
+    )(gated_f, gated_r, out_gain[None], w_out)
 
 
 def direction_terms(values, b_blk, scores, steps_dt, rates, reverse):
@@ -66,20 +340,14 @@
     dt_bias_forward, dt_bias_reverse, rate_forward, rate_reverse,
     skip_forward, skip_reverse, out_gain, w_out,
 ):
-    source = jnp.where(masked[:, None] == 1, mask_embed[None, :], hidden).astype(f32)
-    normed = (
-        source
-        * lax.rsqrt(jnp.mean(source * source, axis=1, keepdims=True) + epsilon)
-        * in_gain[None, :]
-    ).astype(bf16)
-    rows = lax.all_gather(normed, "head", axis=0, tiled=True)
-    gate_act = jax.nn.silu(dot(rows, w_gate))
-    step_proj = dot(rows, w_step)
+    n = lax.axis_size("head")
+    gate_act, values, step_proj, bc = project(
+        n, hidden, masked, mask_embed, in_gain, w_gate, w_value, w_step, w_bc
+    )
     row_count, head_count = step_proj.shape
     block_count = row_count // BLOCK
-    values = jax.nn.silu(dot(rows, w_value)).astype(bf16)
     values = values.reshape(block_count, BLOCK, head_count, HEAD_DIM)
-    bc = dot(rows, w_bc).astype(bf16).reshape(block_count, BLOCK, 2 * STATE)
+    bc = bc.reshape(block_count, BLOCK, 2 * STATE)
     b_blk, c_blk = bc[..., :STATE], bc[..., STATE:]
     scores = jnp.einsum("btn,bsn->bts", c_blk, b_blk, preferred_element_type=f32)
     dt_f = jax.nn.softplus(step_proj + dt_bias_forward)
@@ -98,13 +366,7 @@
         carried = jnp.einsum("btn,bhpn->bthp", c_blk, states, preferred_element_type=f32)
         out = inside + carried * jnp.exp(cum)[..., None] + skip[:, None] * values.astype(f32)
         gated.append(out.reshape(row_count, -1) * gate_act)
-    totals = lax.psum(jnp.stack([jnp.sum(g * g, axis=1) for g in gated]), "head")
-    inner = HEADS * HEAD_DIM
-    scale = lax.rsqrt(totals / inner + epsilon)
-    both = gated[0] * scale[0][:, None] + gated[1] * scale[1][:, None]
-    both = (both * out_gain[None, :]).astype(bf16)
-    part = dot(both, w_out).astype(bf16)
-    return lax.psum_scatter(part, "head", scatter_dimension=0, tiled=True)
+    return project_out(n, HEADS * HEAD_DIM, gated[0], gated[1], out_gain, w_out)
 
 
 def solution(mesh):

time: 304 us -> 269 us (0.88)
  Pallas kernels: 0 us -> 165 us
  waiting for transfers between devices: 179 us -> 22.4 us
  matrix products: 49.5 us -> 11.2 us
  blocking collectives: 20.8 us -> 9.09 us
  local copies, waits for them, and re-layouts: 25.5 us -> 31.3 us
    pallas_call x0 -> x2, Pallas kernels: none -> 165 us  [the longest x1 82.8 us: project_out(): pl.pallas_call(functools.partial(output_kernel, n, subs, inner), out_shap...]
    all_gather x1 -> x0, waiting for transfers between devices: 83.5 us -> none  [on_device(): rows = lax.all_gather(normed, 'head', axis=0, tiled=True)]
    reduce_scatter x1 -> x0, waiting for transfers between devices: 74.1 us -> none  [on_device(): return lax.psum_scatter(part, 'head', scatter_dimension=0, tiled=True)]
    dot_general x5 -> x0, matrix products: 38.3 us -> none  [dot(): return jnp.dot(a, b, preferred_element_type=f32)]
    psum x1 -> x0, blocking collectives: 11.7 us -> none  [on_device(): lax.psum(jnp.stack([jnp.sum(g * g, axis=1) for g in gated]), 'head')]
    unnamed x46, local copies, waits for them, and re-layouts: 0.62 us -> 5.14 us
    mul x0 -> x1, other arithmetic: none -> 4.35 us  [on_device(): gated.append(out.reshape(row_count, -1) * gate_act)]
  transfers between devices with their start and end apart: 3 -> 1, of which waited for: 3 -> 1; matrix products, arithmetic and copies ran while one was open for 2% -> 1% of each run, Pallas kernels for 0% -> 0%
where the time goes in v2:
time: 269 us; the launch traced here: 268 us
  Pallas kernels  165 us (61%)
  local copies, waits for them, and re-layouts  31.3 us (12%)
  waiting for transfers between devices  22.4 us (8%)
  other arithmetic  15.4 us (6%)
  between operations  13.7 us (5%)
  matrix products  11.2 us (4%)
  blocking collectives  9.09 us (3%)
    pallas_call x1, Pallas kernels, project_out(): pl.pallas_call(functools.partial(output_kernel, n, subs, inner), out_shap...  82.8 us
    pallas_call x1, Pallas kernels, project(): pl.pallas_call(functools.partial(project_kernel, n, subs), out_shape=(jax...  82.1 us
    all_gather x1, waiting for transfers between devices, on_device(): ends = lax.all_gather(ends, 'seq')  22.4 us
    reshape x4, local copies, waits for them, and re-layouts, on_device(): gated.append(out.reshape(row_count, -1) * gate_act)  17 us
    all_gather x1, blocking collectives, on_device(): logs = lax.all_gather(jnp.stack([terms_f[5], terms_r[5]]), 'seq')  9.09 us
    dot_general x2, matrix products, direction_terms(): jnp.einsum('bhts,bshp->bthp', mixing, values, preferred_element_type=f32)  6.49 us
  transfers between devices with their start and end apart: 1, of which 1 were waited for; matrix products, arithmetic and copies ran while one was open for 1% of the time, Pallas kernels for 0%

profile of v2, /device:TPU:0, one launch (start us, length us, event | category | flops | bytes accessed | tf_op | source)
XLA Modules:
  0.0 268.0 jit_solution(1948448994832308207)
XLA Ops:
  6.5 0.0 all-gather.4.cloned.1.call-start
  6.5 0.7 neg.13
  7.2 1.3 broadcast_in_dim.118.embed
  8.5 1.4 copy.64.masked
  9.9 2.2 copy.65.step_hbm
  12.1 82.1 %shard_map.154 = (bf16[512,1024]{1,0:T(8,128)(2,1)}, bf16[512,1024]{1,0:T(8,128)(2,1)}, f32[512,16]{1,0:T(8,128)}, bf16[512,256]{1,0:T(8,128)(2,1)}) custom-call(bf16[128,4096]{1,0:T(8,128)(2,1)} %hidden.1, s32[128,1]{1,0:T(8,128)} %copy.64.masked, bf16[1,4096]{1,0:T(2,128)(2,1)} %broadcast_in_dim.118.embed, f32[1,4096]{1,0:T(1,128)} %bitcast.93, ...), custom_call_target="tpu_custom_call" | custom-call | tf_op jit(solution)/shard_map/pallas_call | solution.py:144
  94.2 0.0 copy-done.17
  94.2 0.0 copy-done.18
  94.2 1.2 compare_select_fusion
  95.5 0.0 copy-start.1
  95.5 0.0 copy-start.3
  95.5 0.1 copy.67
  95.6 0.3 fusion.38
  95.9 0.2 slice_reduce_fusion.1
  96.0 0.8 slice_reduce_fusion.5
  96.8 0.0 copy-done.19
  96.8 0.1 copy.72
  96.9 0.3 fusion.36
  97.2 0.1 slice_reduce_fusion
  97.2 0.7 slice_reduce_fusion.3
  98.0 0.6 bitcast_exponential_fusion.1
  98.6 0.6 bitcast_exponential_fusion
  99.2 0.0 copy-done.1
  99.2 0.0 copy-done.3
  99.2 2.9 %reshape.268 = bf16[2,256,16,64]{3,2,1,0:T(8,128)(2,1)S(1)} reshape(bf16[512,1024]{1,0:T(8,128)(2,1)} %get-tuple-element.9) | data formatting | bytes 2097152 | tf_op jit(solution)/shard_map/reshape | solution.py:349
  102.1 0.0 copy-start
  102.2 1.7 copy.69
  103.8 0.0 copy-done
  103.9 0.4 fusion.20
  104.3 0.4 fusion.22
  104.7 0.0 copy-start.2
  104.8 0.0 copy-start.13
  104.8 0.0 copy-start.14
  104.8 1.1 fusion.34
  105.8 0.8 pad_maximum_fusion
  106.7 0.0 all-gather.4.cloned.1.call-update
  106.7 0.0 copy-done.4
  106.7 0.7 copy.68
  107.4 0.7 copy.77
  108.1 0.0 copy-done.13
  108.2 9.1 %all-gather.1 = f32[8,2,16]{2,1,0:T(2,128)S(1)} all-gather(f32[1,2,16]{2,1,0:T(2,128)S(1)} %maximum_bitcast_fusion), channel_id=2, replica_groups=mesh['seq'=8,'head'=4] {'seq'}, dimensions={0}, use_global_device_ids=true | all-gather | bytes 1152 | tf_op jit(solution)/shard_map/all_gather | solution.py:358
  117.3 0.6 iota_compare_fusion.1
  118.0 0.1 select_reduce_fusion.1
  118.1 0.1 select_reduce_fusion
  118.2 0.1 exponential_select_fusion.1
  118.3 0.1 exponential_select_fusion
  118.3 1.1 fusion.46
  119.4 22.4 %all-gather.4.cloned.1.call-done = bf16[8,2,16,64,128]{4,3,2,1,0:T(8,128)(2,1)} async-done(((bf16[1,2,16,64,128]{4,3,2,1,0:T(8,128)(2,1)}), bf16[8,2,16,64,128]{4,3,2,1,0:T(8,128)(2,1)}) %all-gather.4.cloned.1.call-update) | async-done | bytes 4194320 | tf_op jit(solution)/shard_map/all_gather | solution.py:359
  141.8 3.5 %fusion.2 = (f32[16,64,128]{2,1,0:T(8,128)}, f32[16,64,128]{2,1,0:T(8,128)S(1)}) fusion(bf16[8,2,16,64,128]{4,3,2,1,0:T(8,128)(2,1)} %all-gather.4.cloned.1.call-done, f32[8,16]{1,0:T(8,128)S(1)} %exponential_select_fusion, f32[8,16]{1,0:T(8,128)S(1)} %exponential_select_fusion.1), kind=kLoop, calls=%fused_computation.5 | loop fusion | flops 6029312 | bytes 5243904 | tf_op jit(solution)/shard_map/reduce_sum | solution.py:335
  145.3 0.5 fusion.26
  145.8 0.5 copy-done.6
  146.4 0.0 copy-done.10
  146.4 2.5 fusion.18
  148.9 3.8 %copy.84 = f32[2,256,16,64]{3,2,1,0:T(8,128)} copy(f32[2,256,16,64]{1,3,2,0:T(8,128)S(1)} %fusion.18) | data formatting | bytes 4194304 | tf_op jit(solution)/shard_map/reshape | solution.py:368
  152.7 3.5 %reshape.266 = f32[512,1024]{1,0:T(8,128)S(1)} reshape(f32[2,256,16,64]{3,2,1,0:T(8,128)} %copy.84) | data formatting | bytes 4194304 | tf_op jit(solution)/shard_map/reshape | solution.py:368
  156.2 0.0 copy-start.21
  156.2 1.7 fusion.27
  158.0 4.0 %fusion.19 = f32[2,256,16,64]{1,3,2,0:T(8,128)} fusion(bf16[2,256,16,64]{1,3,2,0:T(8,128)(2,1)S(1)} %copy.69, f32[2,256,16,64]{1,3,2,0:T(8,128)S(1)} %fusion.27, f32[2,16,256]{2,1,0:T(8,128)S(1)} %copy-done.9, f32[2,16,256]{2,1,0:T(8,128)S(1)} %fusion.36, f32[2,256,256]{2,1,0:T(8,128)S(1)} %copy-done.7, pred[256,256]{1,0:T(8,128)(4,1)S(1)} %iota_compare_fusion, ...), kind=kOutput, calls=%fused_computation.29 | convolution fusion | flops 281542656 | bytes 5931072 | tf_op jit(solution)/shard_map/bhts,bshp->bthp/dot_general | solution.py:310
  161.9 4.8 %copy.85 = f32[2,256,16,64]{3,2,1,0:T(8,128)} copy(f32[2,256,16,64]{1,3,2,0:T(8,128)} %fusion.19) | data formatting | bytes 4194304 | tf_op jit(solution)/shard_map/reshape | solution.py:368
  166.8 5.0 %reshape.267 = f32[512,1024]{1,0:T(8,128)} reshape(f32[2,256,16,64]{3,2,1,0:T(8,128)} %copy.85) | data formatting | bytes 4194304 | tf_op jit(solution)/shard_map/reshape | solution.py:368
  171.7 0.0 copy-done.5
  171.7 4.4 %convert_multiply_fusion.6 = (f32[512,1024]{1,0:T(8,128)}, f32[512,1024]{1,0:T(8,128)}) fusion(f32[512,1024]{1,0:T(8,128)} %reshape.267, bf16[512,1024]{1,0:T(8,128)(2,1)S(1)} %copy-done.5, f32[512,1024]{1,0:T(8,128)S(1)} %reshape.266), kind=kLoop, calls=%fused_computation.24 | loop fusion | flops 1572864 | bytes 9437184 | tf_op jit(solution)/shard_map/mul | solution.py:368
  176.1 82.8 %shard_map.155 = bf16[128,4096]{1,0:T(8,128)(2,1)} custom-call(f32[512,1024]{1,0:T(8,128)} %get-tuple-element.28.gated_f, f32[512,1024]{1,0:T(8,128)} %get-tuple-element.27.gated_r, f32[1,1024]{1,0:T(1,128)} %bitcast.96, bf16[1024,4096]{1,0:T(8,128)(2,1)} %w_hbm.1), custom_call_target="tpu_custom_call" | custom-call | tf_op jit(solution)/shard_map/pallas_call | solution.py:273
  258.9 2.3 copy.93
  (36 shorter events, 0.1 us)
Async XLA Ops:
  6.5 135.3 %all-gather.4.cloned.1.call-start = ((), (), s32[]{:S(2)}) async-start(), calls=%async_computation | async-start | bytes 4718592 | tf_op jit(solution)/shard_map/all_gather | solution.py:359
  12.1 82.1 %copy-start.17 = (f32[16]{0:T(128)S(1)}, f32[16]{0:T(128)}, u32[]{:S(2)}) copy-start(f32[16]{0:T(128)} %param.25) | copy-start | bytes 196
  12.1 82.1 %copy-start.18 = (f32[16]{0:T(128)S(1)}, f32[16]{0:T(128)}, u32[]{:S(2)}) copy-start(f32[16]{0:T(128)} %param.24) | copy-start | bytes 196
  12.1 84.7 %copy-start.19 = (f32[16]{0:T(128)S(1)}, f32[16]{0:T(128)}, u32[]{:S(2)}) copy-start(f32[16]{0:T(128)} %param.27) | copy-start | bytes 196
  95.5 3.7 %copy-start.1 = (f32[512,16]{1,0:T(8,128)}, f32[512,16]{1,0:T(8,128)S(1)}, u32[]{:S(2)}) copy-start(f32[512,16]{1,0:T(8,128)S(1)} %get-tuple-element.29) | copy-start | bytes 98308
  95.5 3.7 %copy-start.3 = (f32[512,16]{1,0:T(8,128)}, f32[512,16]{1,0:T(8,128)S(1)}, u32[]{:S(2)}) copy-start(f32[512,16]{1,0:T(8,128)S(1)} %get-tuple-element.30) | copy-start | bytes 98308
  102.1 1.7 copy-start
  104.7 2.0 copy-start.4
  104.7 2.7 %copy-start.2 = (f32[512,16]{1,0:T(8,128)S(1)}, f32[512,16]{1,0:T(8,128)}, u32[]{:S(2)}) copy-start(f32[512,16]{1,0:T(8,128)} %copy-done.1) | copy-start | bytes 98308
  104.8 3.4 %copy-start.13 = (f32[16]{0:T(128)S(1)}, f32[16]{0:T(128)}, u32[]{:S(2)}) copy-start(f32[16]{0:T(128)} %get-tuple-element.15) | copy-start | bytes 196
  104.8 3.4 %copy-start.14 = (f32[16]{0:T(128)S(1)}, f32[16]{0:T(128)}, u32[]{:S(2)}) copy-start(f32[16]{0:T(128)} %get-tuple-element.19) | copy-start | bytes 196
  104.8 3.4 %copy-start.15 = (f32[16]{0:T(128)S(1)}, f32[16]{0:T(128)}, u32[]{:S(2)}) copy-start(f32[16]{0:T(128)} %get-tuple-element.16) | copy-start | bytes 196
  104.8 3.4 %copy-start.16 = (f32[16]{0:T(128)S(1)}, f32[16]{0:T(128)}, u32[]{:S(2)}) copy-start(f32[16]{0:T(128)} %get-tuple-element.22) | copy-start | bytes 196
  145.3 1.0 copy-start.6
  145.3 1.0 copy-start.8
  145.3 1.0 copy-start.10
  145.3 1.0 copy-start.12
  145.3 1.0 copy-start.20
  156.2 1.8 copy-start.7
  156.2 1.8 copy-start.9
  156.2 1.8 copy-start.11
  156.2 1.8 copy-start.21
  166.8 5.0 %copy-start.5 = (bf16[512,1024]{1,0:T(8,128)(2,1)S(1)}, bf16[512,1024]{1,0:T(8,128)(2,1)}, u32[]{:S(2)}) copy-start(bf16[512,1024]{1,0:T(8,128)(2,1)} %get-tuple-element.12) | copy-start | bytes 3145732
Sparse Core Ops, SparseCore 0:
  106.8 34.9 all-gather.3

commit v3 on v2

--- a/solution.py
+++ b/solution.py
@@ -11,6 +11,7 @@
 HEAD_DIM = 64
 STATE = 128
 BLOCK = 256
+LANES = 128
 
 epsilon = 1e-05
 bf16 = jnp.bfloat16
@@ -291,48 +292,185 @@
     )(gated_f, gated_r, out_gain[None], w_out)
 
 
-def direction_terms(values, b_blk, scores, steps_dt, rates, reverse):
-    block_count, size, head_count, _ = values.shape
-    step_blk = steps_dt.reshape(block_count, size, head_count)
-    logd = -rates * step_blk
-    at = jnp.arange(size)
-    keep = at[:, None] <= at[None, :] if reverse else at[:, None] >= at[None, :]
-    cum = jnp.einsum(
-        "ts,bsh->bth", keep.astype(f32), logd, precision=lax.Precision.HIGHEST
-    )
-    total = cum[:, 0] if reverse else cum[:, -1]
-    cum_h = jnp.swapaxes(cum, 1, 2)
-    differ = cum_h[:, :, :, None] - cum_h[:, :, None, :]
-    weights = (
-        jnp.exp(jnp.where(keep, differ, -jnp.inf)) * jnp.swapaxes(step_blk, 1, 2)[:, :, None, :]
-    )
-    mixing = (scores[:, None] * weights).astype(bf16)
-    inside = jnp.einsum("bhts,bshp->bthp", mixing, values, preferred_element_type=f32)
-    to_end = jnp.exp(total[:, None] - cum) * step_blk
-    scaled = (values.astype(f32) * to_end[..., None]).astype(bf16)
-    states = jnp.einsum("bshp,bsn->bhpn", scaled, b_blk, preferred_element_type=f32)
-    order = range(block_count - 1, -1, -1) if reverse else range(block_count)
-    starts, prefix = [None] * block_count, [None] * block_count
-    running, product = jnp.zeros_like(states[0]), jnp.zeros_like(total[0])
-    for i in order:
-        starts[i], prefix[i] = running, product
-        running = jnp.exp(total[i])[:, None, None] * running + states[i]
-        product = product + total[i]
-    return inside, cum, jnp.stack(starts), jnp.stack(prefix), running, product
-
-
-def entering(gathered, logs, place, reverse):
-    count = gathered.shape[0]
-    at = jnp.arange(count)
-    if reverse:
-        between = (at[None, :] < at[:, None]) & (at[None, :] > place)
-        used = at > place
-    else:
-        between = (at[None, :] > at[:, None]) & (at[None, :] < place)
-        used = at < place
-    decay = jnp.sum(jnp.where(between[:, :, None], logs[None], 0.0), axis=1)
-    factor = jnp.where(used[:, None], jnp.exp(decay), 0.0)
-    return jnp.sum(factor[:, :, None, None] * gathered.astype(f32), axis=0)
+def expand(x, spread):
+    high = x.astype(bf16)
+    return dot(high, spread) + dot((x - high.astype(f32)).astype(bf16), spread)
+
+
+def scan_kernel(
+    count, heads, values, gate, step, bc, params, gated_f, gated_r,
+    cums, cums_t, dts_t, ends_log, states, mine, my_logs, held, logs, enter,
+    send_sem, recv_sem, log_send, log_recv,
+):
+    place = lax.axis_index("seq")
+    rows, units = values.shape
+    blocks = rows // BLOCK
+    lane_of = lax.broadcasted_iota(jnp.int32, (LANES, units), 1)
+    head_of = lax.broadcasted_iota(jnp.int32, (LANES, units), 0) * HEAD_DIM
+    spread = ((lane_of >= head_of) & (lane_of < head_of + HEAD_DIM)).astype(f32).astype(bf16)
+    at_t = lax.broadcasted_iota(jnp.int32, (BLOCK, BLOCK), 0)
+    at_s = lax.broadcasted_iota(jnp.int32, (BLOCK, BLOCK), 1)
+    outs = (gated_f, gated_r)
+
+    def keep(way):
+        return at_t >= at_s if way == 0 else at_t <= at_s
+
+    def rows_of(b):
+        return pl.ds(pl.multiple_of(b * BLOCK, BLOCK), BLOCK)
+
+    @pl.loop(0, blocks)
+    def _(b):
+        at = rows_of(b)
+        val = values[at, :].astype(f32)
+        b_rows = bc[at, 0:STATE]
+        for way in range(2):
+            x = step[at, :] + params[way : way + 1, :]
+            dt = jnp.maximum(x, 0.0) + jnp.log1p(jnp.exp(-jnp.abs(x)))
+            logd = -params[2 + way : 3 + way, :] * dt
+            cum = jnp.dot(
+                keep(way).astype(f32), logd,
+                precision=lax.Precision.HIGHEST, preferred_element_type=f32,
+            )
+            total = cum[BLOCK - 1 : BLOCK, :] if way == 0 else cum[0:1, :]
+            cums[way, b] = cum
+            cums_t[way, b] = cum.T
+            dts_t[way, b] = dt.T
+            ends_log[way, b] = jnp.broadcast_to(total, (8, LANES))
+            scaled = (val * expand(jnp.exp(total - cum) * dt, spread)).astype(bf16)
+            states[way, b] = lax.dot_general(
+                b_rows, scaled, (((0,), (0,)), ((), ())), preferred_element_type=f32
+            )
+
+    for way in range(2):
+        end = states[way, 0 if way == 0 else blocks - 1]
+        log = ends_log[way, 0 if way == 0 else blocks - 1]
+        for i in range(1, blocks):
+            b = i if way == 0 else blocks - 1 - i
+            end = end * expand(jnp.exp(ends_log[way, b]), spread)[0:1] + states[way, b]
+            log = log + ends_log[way, b]
+        mine[way] = end.astype(bf16)
+        my_logs[way] = log
+
+    def send_state(target, slot):
+        way = jnp.where(target > place, 0, 1)
+        return pltpu.make_async_remote_copy(
+            src_ref=mine.at[way], dst_ref=held.at[place], send_sem=send_sem.at[slot],
+            recv_sem=recv_sem.at[place], device_id={"seq": target}, device_id_type=MESH,
+        )
+
+    def send_log(target, slot):
+        way = jnp.where(target > place, 0, 1)
+        return pltpu.make_async_remote_copy(
+            src_ref=my_logs.at[way], dst_ref=logs.at[place], send_sem=log_send.at[slot],
+            recv_sem=log_recv.at[place], device_id={"seq": target}, device_id_type=MESH,
+        )
+
+    def arrive(owner):
+        pltpu.make_async_remote_copy(
+            src_ref=mine.at[0], dst_ref=held.at[owner], send_sem=send_sem.at[0],
+            recv_sem=recv_sem.at[owner], device_id={"seq": owner}, device_id_type=MESH,
+        ).wait_recv()
+        pltpu.make_async_remote_copy(
+            src_ref=my_logs.at[0], dst_ref=logs.at[owner], send_sem=log_send.at[0],
+            recv_sem=log_recv.at[owner], device_id={"seq": owner}, device_id_type=MESH,
+        ).wait_recv()
+
+    line_barrier("seq", count)
+    for other in range(1, count):
+        send_log(lax.rem(place + other, count), other).start()
+        send_state(lax.rem(place + other, count), other).start()
+
+    half = lax.broadcasted_iota(jnp.int32, (BLOCK, 2 * HEAD_DIM), 1) < HEAD_DIM
+
+    @pl.loop(0, blocks)
+    def _(b):
+        at = rows_of(b)
+        scores = lax.dot_general(
+            bc[at, STATE : 2 * STATE], bc[at, 0:STATE], (((1,), (1,)), ((), ())),
+            preferred_element_type=f32,
+        )
+        for way in range(2):
+            masked_scores = jnp.where(keep(way), scores, 0.0)
+            for pair in range(heads // 2):
+                cols = slice(pair * 2 * HEAD_DIM, (pair + 1) * 2 * HEAD_DIM)
+                val = values[at, cols]
+                inside = []
+                for h in (2 * pair, 2 * pair + 1):
+                    differ = cums[way, b, :, h : h + 1] - cums_t[way, b, h : h + 1, :]
+                    weight = jnp.exp(jnp.minimum(differ, 0.0)) * dts_t[way, b, h : h + 1, :]
+                    inside.append(dot((masked_scores * weight).astype(bf16), val))
+                outs[way][at, cols] = jnp.where(half, inside[0], inside[1])
+
+    @pl.loop(0, count)
+    def _(q):
+        @pl.when(q != place)
+        def _():
+            arrive(q)
+
+    enter[...] = jnp.zeros_like(enter)
+
+    def step_in(way, q):
+        factor = expand(jnp.exp(logs[q]), spread)[0:1]
+        enter[way] = enter[way] * factor + held[q].astype(f32)
+
+    @pl.loop(0, count)
+    def _(i):
+        @pl.when(i < place)
+        def _():
+            step_in(0, i)
+
+        @pl.when(count - 1 - i > place)
+        def _():
+            step_in(1, count - 1 - i)
+
+    @pl.loop(0, blocks)
+    def _(i):
+        for way in range(2):
+            b = i if way == 0 else blocks - 1 - i
+            at = rows_of(b)
+            carried = dot(bc[at, STATE : 2 * STATE], enter[way].astype(bf16))
+            skip = expand(jnp.broadcast_to(params[4 + way : 5 + way, :], (8, LANES)), spread)[0:1]
+            out = (
+                outs[way][at, :] + carried * expand(jnp.exp(cums[way, b]), spread)
+                + skip * values[at, :].astype(f32)
+            )
+            outs[way][at, :] = out * gate[at, :].astype(f32)
+            factor = expand(jnp.exp(ends_log[way, b]), spread)[0:1]
+            enter[way] = enter[way] * factor + states[way, b]
+
+    for other in range(1, count):
+        send_state(lax.rem(place + other, count), other).wait_send()
+        send_log(lax.rem(place + other, count), other).wait_send()
+
+
+def scan(count, heads, values, gate, step, bc, params):
+    rows, units = values.shape
+    blocks = rows // BLOCK
+    vmem = pl.BlockSpec(memory_space=pltpu.VMEM)
+    out = jax.ShapeDtypeStruct((rows, units), f32)
+    sems = pltpu.SemaphoreType.DMA((count,))
+    return pl.pallas_call(
+        functools.partial(scan_kernel, count, heads),
+        out_shape=(out, out),
+        in_specs=[vmem] * 5,
+        out_specs=(vmem, vmem),
+        scratch_shapes=[
+            pltpu.VMEM((2, blocks, BLOCK, LANES), f32),
+            pltpu.VMEM((2, blocks, LANES, BLOCK), f32),
+            pltpu.VMEM((2, blocks, LANES, BLOCK), f32),
+            pltpu.VMEM((2, blocks, 8, LANES), f32),
+            pltpu.VMEM((2, blocks, STATE, units), f32),
+            pltpu.VMEM((2, STATE, units), bf16),
+            pltpu.VMEM((2, 8, LANES), f32),
+            pltpu.VMEM((count, STATE, units), bf16),
+            pltpu.VMEM((count, 8, LANES), f32),
+            pltpu.VMEM((2, STATE, units), f32),
+            sems, sems, sems, sems,
+        ],
+        compiler_params=pltpu.CompilerParams(
+            collective_id=2, has_side_effects=True, vmem_limit_bytes=56 * 2**20
+        ),
+    )(values, gate, step, bc, params)
 
 
 def on_device(
@@ -341,32 +479,20 @@
     skip_forward, skip_reverse, out_gain, w_out,
 ):
     n = lax.axis_size("head")
+    heads = w_step.shape[1]
+    more = LANES - heads
     gate_act, values, step_proj, bc = project(
-        n, hidden, masked, mask_embed, in_gain, w_gate, w_value, w_step, w_bc
+        n, hidden, masked, mask_embed, in_gain, w_gate, w_value,
+        jnp.pad(w_step, ((0, 0), (0, more))), w_bc,
     )
-    row_count, head_count = step_proj.shape
-    block_count = row_count // BLOCK
-    values = values.reshape(block_count, BLOCK, head_count, HEAD_DIM)
-    bc = bc.reshape(block_count, BLOCK, 2 * STATE)
-    b_blk, c_blk = bc[..., :STATE], bc[..., STATE:]
-    scores = jnp.einsum("btn,bsn->bts", c_blk, b_blk, preferred_element_type=f32)
-    dt_f = jax.nn.softplus(step_proj + dt_bias_forward)
-    dt_r = jax.nn.softplus(step_proj + dt_bias_reverse)
-    terms_f = direction_terms(values, b_blk, scores, dt_f, rate_forward, False)
-    terms_r = direction_terms(values, b_blk, scores, dt_r, rate_reverse, True)
-    ends = jnp.stack([terms_f[4], terms_r[4]]).astype(bf16)
-    logs = lax.all_gather(jnp.stack([terms_f[5], terms_r[5]]), "seq")
-    ends = lax.all_gather(ends, "seq")
-    place = lax.axis_index("seq")
-    gated = []
-    for i, (terms, skip) in enumerate(((terms_f, skip_forward), (terms_r, skip_reverse))):
-        inside, cum, starts, prefix = terms[:4]
-        enter = entering(ends[:, i], logs[:, i], place, i == 1)
-        states = (starts + jnp.exp(prefix)[:, :, None, None] * enter[None]).astype(bf16)
-        carried = jnp.einsum("btn,bhpn->bthp", c_blk, states, preferred_element_type=f32)
-        out = inside + carried * jnp.exp(cum)[..., None] + skip[:, None] * values.astype(f32)
-        gated.append(out.reshape(row_count, -1) * gate_act)
-    return project_out(n, HEADS * HEAD_DIM, gated[0], gated[1], out_gain, w_out)
+    params = jnp.stack(
+        [dt_bias_forward, dt_bias_reverse, rate_forward, rate_reverse, skip_forward, skip_reverse]
+    )
+    params = jnp.pad(params, ((0, 2), (0, more)))
+    gated_f, gated_r = scan(
+        lax.axis_size("seq"), heads, values, gate_act, step_proj, bc, params
+    )
+    return project_out(n, HEADS * HEAD_DIM, gated_f, gated_r, out_gain, w_out)
 
 
 def solution(mesh):

time: 269 us -> 210 us (0.78)
  Pallas kernels: 165 us -> 198 us
  local copies, waits for them, and re-layouts: 31.3 us -> 8.87 us
  waiting for transfers between devices: 22.4 us -> 0 us
  other arithmetic: 15.4 us -> 0 us
  between operations: 13.7 us -> 0.03 us
  matrix products: 11.2 us -> 0 us
  blocking collectives: 9.09 us -> 0 us
    pallas_call x0 -> x1, Pallas kernels: none -> 36.7 us  [scan(): pl.pallas_call(functools.partial(scan_kernel, count, heads), out_shape=(o...]
    all_gather x1 -> x0, waiting for transfers between devices: 22.4 us -> none  [on_device(): ends = lax.all_gather(ends, 'seq')]
    reshape x8 -> x0, local copies, waits for them, and re-layouts: 21.8 us -> none  [the longest x4 17 us: on_device(): gated.append(out.reshape(row_count, -1) * gate_act)]
    dot_general x9 -> x0, matrix products: 11.2 us -> none  [the longest x2 6.49 us: direction_terms(): jnp.einsum('bhts,bshp->bthp', mixing, values, preferred_element_type=f32)]
    all_gather x1 -> x0, blocking collectives: 9.09 us -> none  [on_device(): logs = lax.all_gather(jnp.stack([terms_f[5], terms_r[5]]), 'seq')]
    mul x1 -> x0, other arithmetic: 4.35 us -> none  [on_device(): gated.append(out.reshape(row_count, -1) * gate_act)]
    pallas_call x1, Pallas kernels: 82.8 us -> 79 us  [project_out(): pl.pallas_call(functools.partial(output_kernel, n, subs, inner), out_shap...]
    reduce_sum x3 -> x0, other arithmetic: 3.7 us -> none  [the longest x1 3.53 us: entering(): return jnp.sum(factor[:, :, None, None] * gathered.astype(f32), axis=0)]
  transfers between devices with their start and end apart: 1 -> 0, of which waited for: 1 -> 0; matrix products, arithmetic and copies ran while one was open for 1% -> 0% of each run, Pallas kernels for 0% -> 0%
where the time goes in v3:
time: 210 us; the launch traced here: 207 us
  Pallas kernels  198 us (94%)
  local copies, waits for them, and re-layouts  8.87 us (4%)
    pallas_call x1, Pallas kernels, project(): pl.pallas_call(functools.partial(project_kernel, n, subs), out_shape=(jax...  82 us
    pallas_call x1, Pallas kernels, project_out(): pl.pallas_call(functools.partial(output_kernel, n, subs, inner), out_shap...  79 us
    pallas_call x1, Pallas kernels, scan(): pl.pallas_call(functools.partial(scan_kernel, count, heads), out_shape=(o...  36.7 us

profile of v3, /device:TPU:0, one launch (start us, length us, event | category | flops | bytes accessed | tf_op | source)
XLA Modules:
  0.0 206.6 jit_solution(455889453023214688)
XLA Ops:
  0.0 0.8 stack.27
  0.8 0.6 pad.9.params
  1.3 1.3 broadcast_in_dim.13.embed
  2.7 1.4 copy.18.masked
  4.0 1.4 copy.17
  5.4 1.2 pad.8.step_hbm
  6.6 82.0 %shard_map.154 = (bf16[512,1024]{1,0:T(8,128)(2,1)}, bf16[512,1024]{1,0:T(8,128)(2,1)}, f32[512,128]{1,0:T(8,128)}, bf16[512,256]{1,0:T(8,128)(2,1)}) custom-call(bf16[128,4096]{1,0:T(8,128)(2,1)} %hidden.1, s32[128,1]{1,0:T(8,128)} %copy.18.masked, bf16[1,4096]{1,0:T(2,128)(2,1)} %broadcast_in_dim.13.embed, f32[1,4096]{1,0:T(1,128)} %bitcast.9, ...), custom_call_target="tpu_custom_call" | custom-call | tf_op jit(solution)/shard_map/pallas_call | solution.py:145
  88.6 36.7 %shard_map.155 = (f32[512,1024]{1,0:T(8,128)}, f32[512,1024]{1,0:T(8,128)}) custom-call(bf16[512,1024]{1,0:T(8,128)(2,1)} %get-tuple-element.11.values, bf16[512,1024]{1,0:T(8,128)(2,1)} %get-tuple-element.12.gate, f32[512,128]{1,0:T(8,128)} %get-tuple-element.13.step, bf16[512,256]{1,0:T(8,128)(2,1)} %get-tuple-element.14.bc, f32[8,128]{1,0:T(8,128)} %pad.9.params), custom_call_target="tpu_custom_call" | custom-call | tf_op jit(solution)/shard_map/pallas_call | solution.py:452
  125.3 79.0 %shard_map.156 = bf16[128,4096]{1,0:T(8,128)(2,1)} custom-call(f32[512,1024]{1,0:T(8,128)} %get-tuple-element.15.gated_f, f32[512,1024]{1,0:T(8,128)} %get-tuple-element.16.gated_r, f32[1,1024]{1,0:T(1,128)} %bitcast.10, bf16[1024,4096]{1,0:T(8,128)(2,1)} %w_hbm.1), custom_call_target="tpu_custom_call" | custom-call | tf_op jit(solution)/shard_map/pallas_call | solution.py:274
  204.3 2.3 %copy.20 = bf16[128,4096]{1,0:T(8,128)(2,1)} copy(bf16[128,4096]{1,0:T(8,128)(2,1)} %shard_map.156) | data formatting | bytes 2097152

commit v4 on v3

--- a/solution.py
+++ b/solution.py
@@ -96,18 +96,18 @@
 
     @pl.loop(1, n)
     def _(d):
-        @pl.when(me - d >= 0)
-        def _():
-            for sub in range(subs):
+        for sub in range(subs):
+
+            @pl.when(me - d >= 0)
+            def _():
                 copy(me - d, sub, right_sem, me).wait_recv()
 
                 @pl.when(me < n - 1)
                 def _():
                     copy(me - d, sub, right_sem, me + 1).start()
 
-        @pl.when(me + d < n)
-        def _():
-            for sub in range(subs):
+            @pl.when(me + d < n)
+            def _():
                 copy(me + d, sub, left_sem, me).wait_recv()
 
                 @pl.when(me > 0)
@@ -138,7 +138,7 @@
 def project(n, hidden, masked, mask_embed, in_gain, w_gate, w_value, w_step, w_bc):
     count, width = hidden.shape
     units, heads, both = w_gate.shape[1], w_step.shape[1], w_bc.shape[1]
-    subs = 2
+    subs = 4
     total = n * count
     vmem, any_ = pl.BlockSpec(memory_space=pltpu.VMEM), pl.BlockSpec(memory_space=pl.ANY)
     sems = pltpu.SemaphoreType.DMA((n, subs))
@@ -173,14 +173,11 @@
     load.start()
     count = out.shape[0]
     part = out.shape[1] // subs
-    ones = jnp.ones((8, gated_f.shape[1]), f32)
 
     def row_sums(ref):
         g = ref[...]
-        return lax.dot_general(
-            ones, g * g, (((1,), (1,)), ((), ())),
-            precision=lax.Precision.HIGHEST, preferred_element_type=f32,
-        )
+        total = jnp.sum(g * g, axis=1, keepdims=True)
+        return jnp.broadcast_to(total, (total.shape[0], LANES)).T[0:8]
 
     sums[me, 0:8, :] = row_sums(gated_f)
     sums[me, 8:16, :] = row_sums(gated_r)

time: 210 us -> 206 us (0.981)
  Pallas kernels: 198 us -> 193 us
    pallas_call x1, Pallas kernels: 79 us -> 76.1 us  [project_out(): pl.pallas_call(functools.partial(output_kernel, n, subs, inner), out_shap...]
where the time goes in v4:
time: 206 us; the launch traced here: 202 us
  Pallas kernels  193 us (94%)
  local copies, waits for them, and re-layouts  8.87 us (4%)
    pallas_call x1, Pallas kernels, project(): pl.pallas_call(functools.partial(project_kernel, n, subs), out_shape=(jax...  80.8 us
    pallas_call x1, Pallas kernels, project_out(): pl.pallas_call(functools.partial(output_kernel, n, subs, inner), out_shap...  76.1 us
    pallas_call x1, Pallas kernels, scan(): pl.pallas_call(functools.partial(scan_kernel, count, heads), out_shape=(o...  36.5 us

profile of v4, /device:TPU:0, one launch (start us, length us, event | category | flops | bytes accessed | tf_op | source)
XLA Modules:
  0.0 202.3 jit_solution(4985697144214257526)
XLA Ops:
  0.0 0.8 stack.27
  0.8 0.6 pad.9.params
  1.3 1.3 broadcast_in_dim.13.embed
  2.7 1.4 copy.18.masked
  4.0 1.4 copy.17
  5.4 1.2 pad.8.step_hbm
  6.6 80.8 %shard_map.154 = (bf16[512,1024]{1,0:T(8,128)(2,1)}, bf16[512,1024]{1,0:T(8,128)(2,1)}, f32[512,128]{1,0:T(8,128)}, bf16[512,256]{1,0:T(8,128)(2,1)}) custom-call(bf16[128,4096]{1,0:T(8,128)(2,1)} %hidden.1, s32[128,1]{1,0:T(8,128)} %copy.18.masked, bf16[1,4096]{1,0:T(2,128)(2,1)} %broadcast_in_dim.13.embed, f32[1,4096]{1,0:T(1,128)} %bitcast.9, ...), custom_call_target="tpu_custom_call" | custom-call | tf_op jit(solution)/shard_map/pallas_call | solution.py:145
  87.4 36.5 %shard_map.155 = (f32[512,1024]{1,0:T(8,128)}, f32[512,1024]{1,0:T(8,128)}) custom-call(bf16[512,1024]{1,0:T(8,128)(2,1)} %get-tuple-element.11.values, bf16[512,1024]{1,0:T(8,128)(2,1)} %get-tuple-element.12.gate, f32[512,128]{1,0:T(8,128)} %get-tuple-element.13.step, bf16[512,256]{1,0:T(8,128)(2,1)} %get-tuple-element.14.bc, f32[8,128]{1,0:T(8,128)} %pad.9.params), custom_call_target="tpu_custom_call" | custom-call | tf_op jit(solution)/shard_map/pallas_call | solution.py:449
  123.9 76.1 %shard_map.156 = bf16[128,4096]{1,0:T(8,128)(2,1)} custom-call(f32[512,1024]{1,0:T(8,128)} %get-tuple-element.15.gated_f, f32[512,1024]{1,0:T(8,128)} %get-tuple-element.16.gated_r, f32[1,1024]{1,0:T(1,128)} %bitcast.10, bf16[1024,4096]{1,0:T(8,128)(2,1)} %w_hbm.1), custom_call_target="tpu_custom_call" | custom-call | tf_op jit(solution)/shard_map/pallas_call | solution.py:271
  200.1 2.3 %copy.20 = bf16[128,4096]{1,0:T(8,128)(2,1)} copy(bf16[128,4096]{1,0:T(8,128)(2,1)} %shard_map.156) | data formatting | bytes 2097152
